TPU v7x, 128 devices: a whole 4x4x4 slice. The times are simulated.
128 devices in a mesh: pool: 4 (over y), fft: 32 (over z, x, core).
Axes of the slice: x: 4, y: 4, z: 4, core: 2. Of those that a mesh axis runs over, the one named last changes fastest.
Arguments:
- wave_coeff: float32 [4, 2, 2, 128, 128, 128], P('pool', None, None, None, 'fft'), may hold values from -16384 to 16384, as said below
- band_energy: float32 [4, 2], P('pool'), may hold values from -1 to -0.25
- local_potential: float32 [128, 128, 128], P('fft'), may hold values from 0 to 1
- perturbation: float32 [128, 128, 128], P('fft'), may hold values from -6 to 6
- xc_kernel: float32 [128, 128, 128], P('fft'), may hold values from -2 to -0.5
Outputs:
- response_coeff: float32 [4, 2, 2, 128, 128, 128], P('pool', None, None, None, 'fft')
- response_density: float32 [128, 128, 128], P('fft')
- hxc_potential: float32 [128, 128, 128], P('fft')
Inputs may be any that keep to these rules, and one draw needn't show every extreme that they name: `wave_coeff`: each band has <psi|psi> = 1.
All inputs are finite; a program needn't handle non-finite values.
Results may differ from a plain program's by a relative error of at most 0.0003.
Values sent between devices are 32-bit elements; how exact they have to be, the bound alone decides.
A program may use at most 128 MiB of HBM per device.

v0:
```python
import math

import jax
import jax.numpy as jnp
from jax import lax
from jax.sharding import PartitionSpec as P

NX = 128
NY = 128
NZ = 128
CG_STEPS = 3


cell_length = 51.3
projector_shift = 2.0
precondition_shift = 1.0
highest = lax.Precision.HIGHEST


def wavenumbers(position, length):
    signed = jnp.where(2 * position >= length, position - length, position)
    return signed.astype(jnp.float32) * (2.0 * math.pi / cell_length)


def point_offset(point, axis_number):
    bit_value = point // 2**axis_number % 2
    return (0.5 * bit_value.astype(jnp.float32) - 0.25) * (2.0 * math.pi / cell_length)


def dft_tables(length, inverse):
    position = jnp.arange(length, dtype=jnp.int32)
    product = position[:, None] * position[None, :] % length
    phases = product.astype(jnp.float32) * (2.0 * math.pi / length)
    orientation = 1.0 if inverse else -1.0
    return (jnp.cos(phases), orientation * jnp.sin(phases))


def transform(real_part, imag_part, pattern, length, inverse):
    cosine, sine_table = dft_tables(length, inverse)

    def contract(operand, matrix):
        return jnp.einsum(
            pattern, operand, matrix, precision=highest, preferred_element_type=jnp.float32
        )

    out_real = contract(real_part, cosine) - contract(imag_part, sine_table)
    out_imag = contract(real_part, sine_table) + contract(imag_part, cosine)
    return (out_real, out_imag)


def to_real(real_part, imag_part):
    real_part, imag_part = transform(
        real_part, imag_part, "bxyz,zw->bxyw", real_part.shape[3], True
    )
    real_part, imag_part = transform(
        real_part, imag_part, "bxyz,xw->bwyz", real_part.shape[1], True
    )

    def finish_rows(pieces):
        part_real, part_imag = pieces
        factor = 1.0 / (NX * NY * NZ)
        part_real, part_imag = transform(
            part_real, part_imag, "bxyz,yw->bxwz", part_real.shape[2], True
        )
        return (part_real * factor, part_imag * factor)

    return finish_rows(
        (
            lax.all_to_all(real_part, "fft", split_axis=1, concat_axis=2, tiled=True),
            lax.all_to_all(imag_part, "fft", split_axis=1, concat_axis=2, tiled=True),
        )
    )


def to_reciprocal(real_part, imag_part):
    real_part, imag_part = transform(
        real_part, imag_part, "bxyz,yw->bxwz", real_part.shape[2], False
    )

    def finish_rows(pieces):
        part_real, part_imag = pieces
        part_real, part_imag = transform(
            part_real, part_imag, "bxyz,xw->bwyz", part_real.shape[1], False
        )
        part_real, part_imag = transform(
            part_real, part_imag, "bxyz,zw->bxyw", part_real.shape[3], False
        )
        return (part_real, part_imag)

    return finish_rows(
        (
            lax.all_to_all(real_part, "fft", split_axis=2, concat_axis=1, tiled=True),
            lax.all_to_all(imag_part, "fft", split_axis=2, concat_axis=1, tiled=True),
        )
    )


def spread(values):
    return values[:, None, None, None]


def body(wave_coeff, band_energy, local_potential, perturbation, xc_kernel):
    points, bands = band_energy.shape
    batch_size = points * bands
    local_y = wave_coeff.shape[4]
    grid_total = NX * NY * NZ
    column = lax.axis_index("fft") * local_y + jnp.arange(local_y, dtype=jnp.int32)
    point_ids = lax.axis_index("pool") * points + jnp.arange(points, dtype=jnp.int32)
    base_x = wavenumbers(jnp.arange(NX, dtype=jnp.int32), NX)
    base_y = wavenumbers(column, NY)
    base_z = wavenumbers(jnp.arange(NZ, dtype=jnp.int32), NZ)
    kinetic = 0.5 * (
        base_x[:, None, None] ** 2 + base_y[None, :, None] ** 2 + base_z[None, None, :] ** 2
    )
    point_x = (base_x[None, :] + point_offset(point_ids, 0)[:, None]) ** 2
    point_y = (base_y[None, :] + point_offset(point_ids, 1)[:, None]) ** 2
    point_z = (base_z[None, :] + point_offset(point_ids, 2)[:, None]) ** 2
    point_kinetic = 0.5 * (
        point_x[:, :, None, None] + point_y[:, None, :, None] + point_z[:, None, None, :]
    )
    full_shape = (points, bands, NX, local_y, NZ)
    shifted = (point_kinetic[:, None] - band_energy[:, :, None, None, None]).reshape(
        batch_size, NX, local_y, NZ
    )
    precond = jnp.broadcast_to(
        (1.0 / (point_kinetic + precondition_shift))[:, None], full_shape
    ).reshape(batch_size, NX, local_y, NZ)
    wave_real = wave_coeff[:, :, 0].reshape(batch_size, NX, local_y, NZ)
    wave_imag = wave_coeff[:, :, 1].reshape(batch_size, NX, local_y, NZ)
    flat_wave_real = wave_real.reshape(points, bands, -1)
    flat_wave_imag = wave_imag.reshape(points, bands, -1)

    def local_products(field_real, field_imag):
        flat_real = field_real.reshape(points, bands, -1)
        flat_imag = field_imag.reshape(points, bands, -1)
        pattern = "kml,knl->kmn"
        prod_real = jnp.einsum(
            pattern,
            flat_wave_real,
            flat_real,
            precision=highest,
            preferred_element_type=jnp.float32,
        )
        prod_real = prod_real + jnp.einsum(
            pattern,
            flat_wave_imag,
            flat_imag,
            precision=highest,
            preferred_element_type=jnp.float32,
        )
        prod_imag = jnp.einsum(
            pattern,
            flat_wave_real,
            flat_imag,
            precision=highest,
            preferred_element_type=jnp.float32,
        )
        prod_imag = prod_imag - jnp.einsum(
            pattern,
            flat_wave_imag,
            flat_real,
            precision=highest,
            preferred_element_type=jnp.float32,
        )
        return (prod_real / grid_total, prod_imag / grid_total)

    def project(prod_real, prod_imag):
        pattern = "kmn,kml->knl"
        out_real = jnp.einsum(
            pattern,
            prod_real,
            flat_wave_real,
            precision=highest,
            preferred_element_type=jnp.float32,
        )
        out_real = out_real - jnp.einsum(
            pattern,
            prod_imag,
            flat_wave_imag,
            precision=highest,
            preferred_element_type=jnp.float32,
        )
        out_imag = jnp.einsum(
            pattern,
            prod_imag,
            flat_wave_real,
            precision=highest,
            preferred_element_type=jnp.float32,
        )
        out_imag = out_imag + jnp.einsum(
            pattern,
            prod_real,
            flat_wave_imag,
            precision=highest,
            preferred_element_type=jnp.float32,
        )
        return (out_real.reshape(wave_real.shape), out_imag.reshape(wave_real.shape))

    def inner_local(left_real, left_imag, right_real, right_imag):
        return jnp.sum(left_real * right_real + left_imag * right_imag, axis=(1, 2, 3)) / grid_total

    def product_sum(field_real, field_imag):
        return lax.psum(local_products(field_real, field_imag), "fft")

    space_wave_real, space_wave_imag = to_real(wave_real, wave_imag)
    mixed_real, mixed_imag = to_reciprocal(
        perturbation * space_wave_real, perturbation * space_wave_imag
    )
    prod_real, prod_imag = product_sum(mixed_real, mixed_imag)
    proj_real, proj_imag = project(prod_real, prod_imag)
    resid_real = proj_real - mixed_real
    resid_imag = proj_imag - mixed_imag
    solution_real = jnp.zeros_like(resid_real)
    solution_imag = jnp.zeros_like(resid_imag)
    step_real = precond * resid_real
    step_imag = precond * resid_imag

    def residual_sum(left_real, left_imag, right_real, right_imag):
        return lax.psum(inner_local(left_real, left_imag, right_real, right_imag), "fft")

    search_real, search_imag = (step_real, step_imag)
    residual_dot = residual_sum(resid_real, resid_imag, step_real, step_imag)
    for iteration in range(CG_STEPS):
        space_real, space_imag = to_real(search_real, search_imag)
        pot_real, pot_imag = to_reciprocal(
            local_potential * space_real, local_potential * space_imag
        )
        image_real = shifted * search_real + pot_real
        image_imag = shifted * search_imag + pot_imag
        image_real, image_imag, space_real, space_imag = (
            image_real,
            image_imag,
            space_real,
            space_imag,
        )
        prod_real, prod_imag = product_sum(search_real, search_imag)
        back_real, back_imag = project(prod_real, prod_imag)
        image_real = image_real + projector_shift * back_real
        image_imag = image_imag + projector_shift * back_imag
        curvature = lax.psum(inner_local(search_real, search_imag, image_real, image_imag), "fft")
        step_size = residual_dot / curvature
        solution_real = solution_real + spread(step_size) * search_real
        solution_imag = solution_imag + spread(step_size) * search_imag
        resid_real = resid_real - spread(step_size) * image_real
        resid_imag = resid_imag - spread(step_size) * image_imag
        if iteration + 1 < CG_STEPS:
            step_real = precond * resid_real
            step_imag = precond * resid_imag
            dot_new = residual_sum(resid_real, resid_imag, step_real, step_imag)
            ratio = dot_new / residual_dot
            search_real = step_real + spread(ratio) * search_real
            search_imag = step_imag + spread(ratio) * search_imag
            residual_dot = dot_new
    response_real, response_imag = to_real(solution_real, solution_imag)
    density_local = (
        2.0
        * grid_total
        * jnp.sum(space_wave_real * response_real + space_wave_imag * response_imag, axis=0)
    )
    response_density = lax.psum(density_local, "pool")
    squared = 2.0 * kinetic
    nonzero = (squared > 0).astype(jnp.float32)
    coulomb = 4.0 * math.pi * nonzero / (squared + (1.0 - nonzero))
    hart_real, hart_imag = to_reciprocal(
        response_density[None], jnp.zeros_like(response_density)[None]
    )
    back_real, back_imag = to_real(coulomb * hart_real, coulomb * hart_imag)
    hxc_potential = back_real[0] + xc_kernel * response_density
    response_coeff = jnp.stack([solution_real, solution_imag], axis=1).reshape(wave_coeff.shape)
    return (response_coeff, response_density, hxc_potential)


def solution(mesh):
    return jax.shard_map(
        body,
        mesh=mesh,
        in_specs=(
            P("pool", None, None, None, "fft", None),
            P("pool", None),
            P("fft", None, None),
            P("fft", None, None),
            P("fft", None, None),
        ),
        out_specs=(
            P("pool", None, None, None, "fft", None),
            P("fft", None, None),
            P("fft", None, None),
        ),
        check_vma=False,
    )
```

profile of v0, /device:TPU:1, one launch (start us, length us, event | category | flops | bytes accessed | tf_op | source)
XLA Modules:
  0.0 1242.8 jit_solution(13218956259743617528)
XLA Ops:
  14.8 9.4 all-to-all-start
  27.3 8.4 all-to-all-done
  35.8 5.3 all-to-all-start.1
  42.9 9.7 all-to-all-done.1
  58.3 4.0 all-to-all-start.2
  65.3 8.8 all-to-all-done.2
  74.8 4.8 all-to-all-start.3
  83.3 7.9 all-to-all-done.3
  99.7 5.1 fusion.975
  104.8 4.9 fusion.977
  109.7 5.0 fusion.82
  114.7 4.9 fusion.84
  119.6 62.9 %all-reduce.4 = (f32[2,2]{0,1:T(2,128)S(1)}, f32[2,2]{0,1:T(2,128)S(1)}) all-reduce(f32[2,2]{0,1:T(2,128)S(1)} %fusion.82, f32[2,2]{0,1:T(2,128)S(1)} %fusion.84), channel_id=1, replica_groups=mesh['pool'=4,'fft'=32] {'fft'}, use_global_device_ids=true, to_apply=%region_0.1 | all-reduce | flops 8 | bytes 64 | tf_op jit(solution)/shard_map/psum | solution.py:203
  208.0 6.6 all-to-all-start.4
  219.8 5.9 fusion.981
  228.0 6.0 fusion.979
  234.0 4.9 fusion.88
  239.0 5.2 fusion.86
  245.3 62.6 %all-reduce.3 = (f32[2,2]{0,1:T(2,128)S(1)}, f32[2,2]{0,1:T(2,128)S(1)}) all-reduce(f32[2,2]{0,1:T(2,128)S(1)} %fusion.88, f32[2,2]{0,1:T(2,128)S(1)} %fusion.86), channel_id=1, replica_groups=mesh['pool'=4,'fft'=32] {'fft'}, use_global_device_ids=true, to_apply=%region_5.6 | all-reduce | flops 8 | bytes 64 | tf_op jit(solution)/shard_map/psum | solution.py:203
  312.5 10.1 all-to-all-start.5
  329.7 4.5 all-to-all-done.5
  341.0 4.7 all-to-all-start.6
  349.7 7.7 all-to-all-done.6
  357.4 5.0 all-to-all-start.7
  362.4 3.9 fusion.4
  384.4 62.6 %all-reduce.2 = (f32[2]{0:T(128)S(1)}, f32[2]{0:T(128)S(1)}) all-reduce(f32[2]{0:T(128)S(1)} %broadcast_multiply_fusion.41, f32[2]{0:T(128)S(1)} %broadcast_multiply_fusion.40), channel_id=1, replica_groups=mesh['pool'=4,'fft'=32] {'fft'}, use_global_device_ids=true, to_apply=%region_3.4 | all-reduce | flops 4 | bytes 32 | tf_op jit(solution)/shard_map/psum | solution.py:219
  449.8 67.6 %psum.111 = f32[2]{0:T(128)S(1)} all-reduce(f32[2]{0:T(128)S(1)} %broadcast_multiply_fusion.39), channel_id=1, replica_groups=mesh['pool'=4,'fft'=32] {'fft'}, use_global_device_ids=true, to_apply=%region_9.10 | all-reduce | flops 2 | bytes 16 | tf_op jit(solution)/shard_map/psum | solution.py:219
  528.9 5.3 all-to-all-start.8
  539.3 5.9 fusion.983
  547.5 6.0 fusion.985
  553.6 5.0 fusion.90
  558.6 5.0 fusion.92
  564.8 62.6 %all-reduce.1 = (f32[2,2]{0,1:T(2,128)S(1)}, f32[2,2]{0,1:T(2,128)S(1)}) all-reduce(f32[2,2]{0,1:T(2,128)S(1)} %fusion.90, f32[2,2]{0,1:T(2,128)S(1)} %fusion.92), channel_id=1, replica_groups=mesh['pool'=4,'fft'=32] {'fft'}, use_global_device_ids=true, to_apply=%region_10.11 | all-reduce | flops 8 | bytes 64 | tf_op jit(solution)/shard_map/psum | solution.py:203
  632.0 10.0 all-to-all-start.9
  649.0 4.5 all-to-all-done.9
  660.3 4.7 all-to-all-start.10
  668.9 7.7 all-to-all-done.10
  676.7 5.1 all-to-all-start.11
  681.8 3.9 fusion.2
  702.7 62.6 %psum.114 = f32[2]{0:T(128)S(1)} all-reduce(f32[2]{0:T(128)S(1)} %broadcast_multiply_fusion.38), channel_id=1, replica_groups=mesh['pool'=4,'fft'=32] {'fft'}, use_global_device_ids=true, to_apply=%region_13.14 | all-reduce | flops 2 | bytes 16 | tf_op jit(solution)/shard_map/psum | solution.py:240
  767.1 67.8 %psum.115 = f32[2]{0:T(128)S(1)} all-reduce(f32[2]{0:T(128)S(1)} %broadcast_multiply_fusion.37), channel_id=1, replica_groups=mesh['pool'=4,'fft'=32] {'fft'}, use_global_device_ids=true, to_apply=%region_15.16 | all-reduce | flops 2 | bytes 16 | tf_op jit(solution)/shard_map/psum | solution.py:219
  847.0 5.0 all-to-all-start.12
  857.2 5.9 fusion.989
  865.4 6.0 fusion.987
  871.5 4.9 fusion.96
  876.4 5.2 fusion.94
  882.7 62.6 %all-reduce = (f32[2,2]{0,1:T(2,128)S(1)}, f32[2,2]{0,1:T(2,128)S(1)}) all-reduce(f32[2,2]{0,1:T(2,128)S(1)} %fusion.96, f32[2,2]{0,1:T(2,128)S(1)} %fusion.94), channel_id=1, replica_groups=mesh['pool'=4,'fft'=32] {'fft'}, use_global_device_ids=true, to_apply=%region_17.18 | all-reduce | flops 8 | bytes 64 | tf_op jit(solution)/shard_map/psum | solution.py:203
  949.9 10.1 all-to-all-start.13
  966.3 5.3 all-to-all-done.13
  977.7 4.7 all-to-all-start.14
  986.3 7.8 all-to-all-done.14
  994.1 5.0 all-to-all-start.15
  1017.7 62.7 %psum.118 = f32[2]{0:T(128)S(1)} all-reduce(f32[2]{0:T(128)S(1)} %broadcast_multiply_fusion.36), channel_id=1, replica_groups=mesh['pool'=4,'fft'=32] {'fft'}, use_global_device_ids=true, to_apply=%region_19.20 | all-reduce | flops 2 | bytes 16 | tf_op jit(solution)/shard_map/psum | solution.py:240
  1086.8 8.7 all-to-all-start.16
  1098.4 8.8 all-to-all-done.16
  1107.2 4.0 all-to-all-start.17
  1113.5 9.4 all-to-all-done.17
  1126.7 37.2 %all-reduce.7.cloned.1.call-done = f32[4,128,128]{2,1,0:T(8,128)} async-done(((f32[4,128,128]{2,1,0:T(8,128)}), f32[4,128,128]{2,1,0:T(8,128)}) %all-reduce.7.cloned.1.call-update) | async-done | bytes 262160 | tf_op jit(solution)/shard_map/psum | solution.py:260
  1166.9 9.9 all-to-all-start.18
  1178.9 6.9 all-to-all-done.18
  1185.7 4.0 all-to-all-start.19
  1191.2 7.5 all-to-all-done.19
  1213.2 6.8 all-to-all-done.20
  1226.2 6.5 all-to-all-done.21
  (397 shorter events, 276.8 us)
Async XLA Ops:
  14.8 21.0 %all-to-all-start = ((f32[2,128,4,128]{3,2,0,1:T(4,128)}), f32[2,128,4,128]{3,2,0,1:T(4,128)S(1)}, u32[]{:S(2)}, u32[]{:S(2)}) async-start(f32[2,128,4,128]{3,2,0,1:T(4,128)} %copy.168), calls=%async_computation | async-start | bytes 1048576 | tf_op jit(solution)/shard_map/all_to_all | solution.py:69
  26.1 1.2 copy-start.68
  35.8 16.8 %all-to-all-start.1 = ((f32[2,128,4,128]{3,2,0,1:T(4,128)}), f32[2,128,4,128]{3,2,0,1:T(4,128)}, u32[]{:S(2)}, u32[]{:S(2)}) async-start(f32[2,128,4,128]{3,2,0,1:T(4,128)} %copy.172), calls=%async_computation.1 | async-start | bytes 1048576 | tf_op jit(solution)/shard_map/all_to_all | solution.py:70
  54.6 7.8 copy-start.9
  55.5 7.8 copy-start.5
  58.3 15.7 %all-to-all-start.2 = ((f32[2,4,128,128]{3,1,0,2:T(4,128)}), f32[2,4,128,128]{3,1,0,2:T(4,128)S(1)}, u32[]{:S(2)}, u32[]{:S(2)}) async-start(f32[2,4,128,128]{3,1,0,2:T(4,128)} %copy.174), calls=%async_computation.2 | async-start | bytes 1048576 | tf_op jit(solution)/shard_map/all_to_all | solution.py:92
  74.8 16.4 %all-to-all-start.3 = ((f32[2,4,128,128]{3,1,0,2:T(4,128)}), f32[2,4,128,128]{3,1,0,2:T(4,128)}, u32[]{:S(2)}, u32[]{:S(2)}) async-start(f32[2,4,128,128]{3,1,0,2:T(4,128)} %copy.176), calls=%async_computation.3 | async-start | bytes 1048576 | tf_op jit(solution)/shard_map/all_to_all | solution.py:93
  79.8 621.0 %copy-start.2 = (f32[128,4,128]{2,0,1:T(8,128)}, f32[128,4,128]{2,0,1:T(8,128)S(1)}, u32[]{:S(2)}) copy-start(f32[128,4,128]{2,0,1:T(8,128)S(1)} %get-tuple-element.35) | copy-start | bytes 786436
  79.8 685.5 %copy-start.4 = (f32[128,4,128]{2,0,1:T(8,128)}, f32[128,4,128]{2,0,1:T(8,128)S(1)}, u32[]{:S(2)}) copy-start(f32[128,4,128]{2,0,1:T(8,128)S(1)} %get-tuple-element.36) | copy-start | bytes 786436
  80.2 1.3 copy-start.43
  99.7 5.1 copy-start.63
  104.8 4.9 copy-start.50
  114.7 4.9 copy-start.69
  184.4 1.8 copy-start.51
  188.9 2.4 copy-start.52
  208.0 104.5 %all-to-all-start.4 = ((f32[2,128,4,128]{3,2,0,1:T(4,128)}), f32[2,128,4,128]{3,2,0,1:T(4,128)}, u32[]{:S(2)}, u32[]{:S(2)}) async-start(f32[2,128,4,128]{3,2,0,1:T(4,128)} %copy.192), calls=%async_computation.4 | async-start | bytes 1048576 | tf_op jit(solution)/shard_map/all_to_all | solution.py:69
  228.0 6.0 copy-start.53
  228.0 6.0 copy-start.64
  234.0 4.9 copy-start.59
  238.9 5.2 copy-start.29
  308.0 1.8 copy-start.54
  312.5 21.7 %all-to-all-start.5 = ((f32[2,128,4,128]{3,2,0,1:T(4,128)}), f32[2,128,4,128]{3,2,0,1:T(4,128)}, u32[]{:S(2)}, u32[]{:S(2)}) async-start(f32[2,128,4,128]{3,2,0,1:T(4,128)} %copy.194), calls=%async_computation.5 | async-start | bytes 1048576 | tf_op jit(solution)/shard_map/all_to_all | solution.py:70
  341.0 16.4 %all-to-all-start.6 = ((f32[2,4,128,128]{3,1,0,2:T(4,128)}), f32[2,4,128,128]{3,1,0,2:T(4,128)}, u32[]{:S(2)}, u32[]{:S(2)}) async-start(f32[2,4,128,128]{3,1,0,2:T(4,128)} %copy.196), calls=%async_computation.6 | async-start | bytes 1048576 | tf_op jit(solution)/shard_map/all_to_all | solution.py:92
  345.7 2.0 copy-start.17
  357.4 18.1 %all-to-all-start.7 = ((f32[2,4,128,128]{3,1,0,2:T(4,128)}), f32[2,4,128,128]{3,1,0,2:T(4,128)}, u32[]{:S(2)}, u32[]{:S(2)}) async-start(f32[2,4,128,128]{3,1,0,2:T(4,128)} %copy.198), calls=%async_computation.7 | async-start | bytes 1048576 | tf_op jit(solution)/shard_map/all_to_all | solution.py:93
  375.6 1.2 copy-start.38
  381.0 1.4 copy-start.48
  382.4 2.0 copy-start.26
  528.9 103.1 %all-to-all-start.8 = ((f32[2,128,4,128]{3,2,0,1:T(4,128)}), f32[2,128,4,128]{3,2,0,1:T(4,128)}, u32[]{:S(2)}, u32[]{:S(2)}) async-start(f32[2,128,4,128]{3,2,0,1:T(4,128)} %copy.212), calls=%async_computation.8 | async-start | bytes 1048576 | tf_op jit(solution)/shard_map/all_to_all | solution.py:69
  547.5 6.0 copy-start.55
  547.5 6.0 copy-start.65
  553.5 5.0 copy-start.60
  558.6 5.1 copy-start.30
  627.4 1.8 copy-start.56
  632.0 21.5 %all-to-all-start.9 = ((f32[2,128,4,128]{3,2,0,1:T(4,128)}), f32[2,128,4,128]{3,2,0,1:T(4,128)}, u32[]{:S(2)}, u32[]{:S(2)}) async-start(f32[2,128,4,128]{3,2,0,1:T(4,128)} %copy.214), calls=%async_computation.9 | async-start | bytes 1048576 | tf_op jit(solution)/shard_map/all_to_all | solution.py:70
  660.3 16.4 %all-to-all-start.10 = ((f32[2,4,128,128]{3,1,0,2:T(4,128)}), f32[2,4,128,128]{3,1,0,2:T(4,128)}, u32[]{:S(2)}, u32[]{:S(2)}) async-start(f32[2,4,128,128]{3,1,0,2:T(4,128)} %copy.216), calls=%async_computation.10 | async-start | bytes 1048576 | tf_op jit(solution)/shard_map/all_to_all | solution.py:92
  665.0 2.0 copy-start.19
  676.7 18.2 %all-to-all-start.11 = ((f32[2,4,128,128]{3,1,0,2:T(4,128)}), f32[2,4,128,128]{3,1,0,2:T(4,128)}, u32[]{:S(2)}, u32[]{:S(2)}) async-start(f32[2,4,128,128]{3,1,0,2:T(4,128)} %copy.218), calls=%async_computation.11 | async-start | bytes 1048576 | tf_op jit(solution)/shard_map/all_to_all | solution.py:93
  694.9 1.2 copy-start.40
  700.9 1.7 copy-start.13
  836.9 6.1 copy-start
  847.0 102.9 %all-to-all-start.12 = ((f32[2,128,4,128]{3,2,0,1:T(4,128)}), f32[2,128,4,128]{3,2,0,1:T(4,128)}, u32[]{:S(2)}, u32[]{:S(2)}) async-start(f32[2,128,4,128]{3,2,0,1:T(4,128)} %copy.232), calls=%async_computation.12 | async-start | bytes 1048576 | tf_op jit(solution)/shard_map/all_to_all | solution.py:69
  865.4 6.0 copy-start.57
  865.4 6.0 copy-start.66
  871.4 4.9 copy-start.61
  876.3 5.2 copy-start.31
  945.3 1.8 copy-start.58
  949.9 21.7 %all-to-all-start.13 = ((f32[2,128,4,128]{3,2,0,1:T(4,128)}), f32[2,128,4,128]{3,2,0,1:T(4,128)}, u32[]{:S(2)}, u32[]{:S(2)}) async-start(f32[2,128,4,128]{3,2,0,1:T(4,128)} %copy.234), calls=%async_computation.13 | async-start | bytes 1048576 | tf_op jit(solution)/shard_map/all_to_all | solution.py:70
  973.6 1.2 copy-start.34
  977.7 16.4 %all-to-all-start.14 = ((f32[2,4,128,128]{3,1,0,2:T(4,128)}), f32[2,4,128,128]{3,1,0,2:T(4,128)}, u32[]{:S(2)}, u32[]{:S(2)}) async-start(f32[2,4,128,128]{3,1,0,2:T(4,128)} %copy.236), calls=%async_computation.14 | async-start | bytes 1048576 | tf_op jit(solution)/shard_map/all_to_all | solution.py:92
  986.3 12.8 %copy-start.49 = (f32[2,65536]{1,0:T(2,128)S(1)}, f32[2,65536]{1,0:T(2,128)}, u32[]{:S(2)}) copy-start(f32[2,65536]{1,0:T(2,128)} %fusion.988) | copy-start | bytes 1572868
  994.1 16.5 %all-to-all-start.15 = ((f32[2,4,128,128]{3,1,0,2:T(4,128)}), f32[2,4,128,128]{3,1,0,2:T(4,128)}, u32[]{:S(2)}, u32[]{:S(2)}) async-start(f32[2,4,128,128]{3,1,0,2:T(4,128)} %copy.238), calls=%async_computation.15 | async-start | bytes 1048576 | tf_op jit(solution)/shard_map/all_to_all | solution.py:93
  1002.9 2.4 copy-start.62
  1080.7 3.3 copy-start.7
  1086.8 20.4 %all-to-all-start.16 = ((f32[2,128,4,128]{3,2,0,1:T(4,128)}), f32[2,128,4,128]{3,2,0,1:T(4,128)S(1)}, u32[]{:S(2)}, u32[]{:S(2)}) async-start(f32[2,128,4,128]{3,2,0,1:T(4,128)} %copy.252), calls=%async_computation.16 | async-start | bytes 1048576 | tf_op jit(solution)/shard_map/all_to_all | solution.py:69
  1107.2 15.7 %all-to-all-start.17 = ((f32[2,128,4,128]{3,2,0,1:T(4,128)}), f32[2,128,4,128]{3,2,0,1:T(4,128)S(1)}, u32[]{:S(2)}, u32[]{:S(2)}) async-start(f32[2,128,4,128]{3,2,0,1:T(4,128)} %copy.254), calls=%async_computation.17 | async-start | bytes 1048576 | tf_op jit(solution)/shard_map/all_to_all | solution.py:70
  1111.2 52.7 %all-reduce.7.cloned.1.call-start = ((), (), s32[]{:S(2)}) async-start(), calls=%async_computation.22 | async-start | bytes 524288 | tf_op jit(solution)/shard_map/psum | solution.py:260
  1166.9 9.9 copy-start.27
  1166.9 18.8 %all-to-all-start.18 = ((f32[1,4,128,128]{3,1,0,2:T(4,128)}), f32[1,4,128,128]{3,1,0,2:T(4,128)S(1)}, u32[]{:S(2)}, u32[]{:S(2)}) async-start(f32[1,4,128,128]{3,1,0,2:T(4,128)} %copy.256), calls=%async_computation.18 | async-start | bytes 524288 | tf_op jit(solution)/shard_map/all_to_all | solution.py:92
  1185.7 12.9 %all-to-all-start.19 = ((f32[1,4,128,128]{3,1,0,2:T(4,128)}), f32[1,4,128,128]{3,1,0,2:T(4,128)S(1)}, u32[]{:S(2)}, u32[]{:S(2)}) async-start(f32[1,4,128,128]{3,1,0,2:T(4,128)} %copy.258), calls=%async_computation.19 | async-start | bytes 524288 | tf_op jit(solution)/shard_map/all_to_all | solution.py:93
  1207.2 12.8 %all-to-all-start.20 = ((f32[1,128,4,128]{3,2,0,1:T(4,128)}), f32[1,128,4,128]{3,2,0,1:T(4,128)S(1)}, u32[]{:S(2)}, u32[]{:S(2)}) async-start(f32[1,128,4,128]{3,2,0,1:T(4,128)} %copy.268), calls=%async_computation.20 | async-start | bytes 524288 | tf_op jit(solution)/shard_map/all_to_all | solution.py:69
  1212.3 11.5 copy-start.8
  1212.3 11.5 copy-start.12
  1220.0 12.8 %all-to-all-start.21 = ((f32[1,128,4,128]{3,2,0,1:T(4,128)}), f32[1,128,4,128]{3,2,0,1:T(4,128)S(1)}, u32[]{:S(2)}, u32[]{:S(2)}) async-start(f32[1,128,4,128]{3,2,0,1:T(4,128)} %copy.270), calls=%async_computation.21 | async-start | bytes 524288 | tf_op jit(solution)/shard_map/all_to_all | solution.py:70
  (30 other events, 29.6 us)
Sparse Core Ops, SparseCore 0:
  1126.7 37.1 all-reduce.6
where the time goes:
time: 1250 us; the launch traced here: 1240 us
  blocking collectives  574 us (46%)
  matrix products  256 us (20%)
  waiting for transfers between devices  156 us (12%)
  starting transfers between devices  134 us (11%)
  local copies, waits for them, and re-layouts  95.1 us (8%)
  between operations  16.3 us (1%)
    psum x4, blocking collectives, product_sum(): return lax.psum(local_products(field_real, field_imag), 'fft')  251 us
    psum x3, blocking collectives, residual_sum(): lax.psum(inner_local(left_real, left_imag, right_real, right_imag), 'fft')  198 us
    dot_general x130, matrix products, contract(): jnp.einsum(pattern, operand, matrix, precision=highest, preferred_element...  128 us
    psum x2, blocking collectives, body(): lax.psum(inner_local(search_real, search_imag, image_real, image_imag), '...  125 us
    all_to_all x6, starting transfers between devices, to_real(): lax.all_to_all(imag_part, 'fft', split_axis=1, concat_axis=2, tiled=True)  43.3 us
    all_to_all x6, waiting for transfers between devices, to_real(): lax.all_to_all(imag_part, 'fft', split_axis=1, concat_axis=2, tiled=True)  39.9 us
    all_to_all x5, waiting for transfers between devices, to_reciprocal(): lax.all_to_all(real_part, 'fft', split_axis=2, concat_axis=1, tiled=True)  38.9 us
    all_to_all x6, starting transfers between devices, to_real(): lax.all_to_all(real_part, 'fft', split_axis=1, concat_axis=2, tiled=True)  38.8 us
  transfers between devices with their start and end apart: 23, of which 18 were waited for; matrix products, arithmetic and copies ran while one was open for 16% of the time, Pallas kernels for 0%

commit v1 on v0

v1 whole, which is shorter than its diff:
```python
import functools
import math

import jax
import jax.numpy as jnp
import ml_dtypes
import numpy as np
from jax import lax
from jax.experimental import pallas as pl
from jax.experimental.pallas import tpu as pltpu
from jax.sharding import PartitionSpec as P

CG_STEPS = 3
BANDS = 2
cell_length = 51.3
unit = 2.0 * math.pi / cell_length
MESH = pl.DeviceIdType.MESH
f32 = jnp.float32
bf16 = jnp.bfloat16


def left_table(rows, cols, n, sign, scale=1.0):
    rows, cols = np.array(rows), np.array(cols)
    phase = 2.0 * np.pi * ((rows[:, None, 1] * cols[None, :, 1]) % n) / n
    out_part, in_part = rows[:, None, 0], cols[None, :, 0]
    value = np.where(
        out_part == in_part,
        np.cos(phase),
        np.where(out_part == 1, sign, -sign) * np.sin(phase),
    )
    return value * scale


def split_table(table, axis):
    high = table.astype(ml_dtypes.bfloat16)
    low = (table - high.astype(np.float64)).astype(ml_dtypes.bfloat16)
    return np.concatenate([high, high, low], axis=axis)


def real_basis(n, order):
    k = np.array([f for f, _ in order])
    phase = 2.0 * np.pi * ((k[:, None] * np.arange(n)[None, :]) % n) / n
    is_sin = np.array([s for _, s in order])[:, None]
    rows = np.where(is_sin == 1, np.sin(phase), np.cos(phase))
    weight = np.where((k == 0) | (2 * k == n), 1.0, 2.0)[:, None] / n
    return rows, rows * weight


def make_tables(n, parts):
    local = n // parts
    natural = [(c, j) for c in range(2) for j in range(n)]
    by_owner = [(c, q * local + m) for q in range(parts) for c in range(2) for m in range(local)]
    by_local = [(c, q * local + m) for c in range(2) for m in range(local) for q in range(parts)]
    scale = 1.0 / n**3
    left = np.stack(
        [
            split_table(left_table(by_owner, natural, n, 1.0), 1),
            split_table(left_table(natural, by_local, n, 1.0, scale), 1),
            split_table(left_table(by_owner, natural, n, -1.0), 1),
            split_table(left_table(natural, by_local, n, -1.0), 1),
        ]
    )
    right = np.stack(
        [
            split_table(left_table(natural, natural, n, 1.0).T, 0),
            split_table(left_table(natural, natural, n, -1.0).T, 0),
        ]
    )
    half = n // 2
    plain = [(k, 0) for k in range(half + 1)] + [(k, 1) for k in range(1, half)]
    columns = [
        [(2 * p, 0) for p in range(parts)],
        [(half, 0)] + [(2 * p, 1) for p in range(1, parts)],
        [(2 * p + 1, 0) for p in range(parts)],
        [(2 * p + 1, 1) for p in range(parts)],
    ]
    y_rows, y_back = real_basis(n, sum(columns, []))
    rows, back = real_basis(n, plain)
    by_local_x = [q * local + m for m in range(local) for q in range(parts)]
    x_rows = rows[:, by_local_x]
    x_back = np.zeros((parts, 2 * local, n))
    x_back[:, :local] = back.T.reshape(parts, local, n)
    real = [y_rows, y_back.T, x_rows, x_back.reshape(2 * n, n), rows.T, back]
    return left, right, [np.asarray(t, np.float32) for t in real]


def exact_dot(a, b):
    return jnp.dot(a, b, precision=lax.Precision.HIGHEST, preferred_element_type=f32)


def halves(value):
    high = value.astype(bf16)
    low = (value - high.astype(f32)).astype(bf16)
    return high, low


def left_dot(table, data):
    high, low = halves(data)
    return jnp.dot(table, jnp.concatenate([high, low, high], axis=0), preferred_element_type=f32)


def right_dot(data, table):
    high, low = halves(data)
    return jnp.dot(jnp.concatenate([high, low, high], axis=1), table, preferred_element_type=f32)


def kernel(
    n,
    parts,
    pools,
    wave,
    energy,
    potential,
    perturbation,
    xc,
    left,
    right,
    y_rows,
    y_back,
    x_rows,
    x_back,
    z_rows,
    z_back,
    coeff,
    density,
    hxc,
    kin,
    pre,
    resid,
    search,
    space_wave,
    space_search,
    overlap,
    total,
    send,
    recv,
    small_send,
    small_recv,
    pool_send,
    pool_recv,
    pool_dens,
    pool_hart,
    own_dens,
    own_hart,
    go_send,
    go_recv,
    back_send,
    back_recv,
    bulk_out,
    bulk_in,
    small_out,
    small_in,
    pool_out,
    pool_in,
    turn_out,
    turn_in,
):
    local = n // parts
    block = 2 * local * local
    grid_total = n**3
    inverse_total = 1.0 / grid_total
    me = lax.axis_index("fft")
    pool = lax.axis_index("pool")

    def lanes(value, index):
        return value[:, index * n : (index + 1) * n]

    def peer(index):
        return lax.rem(me + index, parts)

    def pool_peer(index):
        return lax.rem(pool + index, pools)

    barrier = pltpu.get_barrier_semaphore()

    def greet(index, _):
        pl.semaphore_signal(barrier, inc=1, device_id={"fft": peer(index)}, device_id_type=MESH)
        return 0

    def greet_pool(index, _):
        pl.semaphore_signal(
            barrier, inc=1, device_id={"pool": pool_peer(index)}, device_id_type=MESH
        )
        return 0

    lax.fori_loop(1, parts, greet, 0)
    lax.fori_loop(1, pools, greet_pool, 0)
    pl.semaphore_wait(barrier, parts + pools - 2)


    def send_bulk(phase, band, value):
        for m in range(local):
            send[phase, band, :, 2 * local * m : 2 * local * (m + 1), :] = lanes(value, m).reshape(
                parts, 2 * local, n
            )
        here = pl.multiple_of(me * block, block)
        recv[phase, band, pl.ds(here, block), :] = send[phase, band, me]

        def start(index, _):
            target = peer(index)
            pltpu.make_async_remote_copy(
                src_ref=send.at[phase, band, target],
                dst_ref=recv.at[phase, band, pl.ds(here, block)],
                send_sem=bulk_out.at[phase, band],
                recv_sem=bulk_in.at[phase, band],
                device_id={"fft": target},
                device_id_type=MESH,
            ).start()
            return 0

        lax.fori_loop(1, parts, start, 0)

    def wait_bytes(ref, sem):
        pltpu.make_async_copy(ref, ref, sem).wait()

    def receive_bulk(phase, band):
        wait_bytes(recv.at[phase, band, pl.ds(0, block * (parts - 1))], bulk_in.at[phase, band])
        rows = []
        for c in range(2):
            for m in range(local):
                pieces = []
                for other in range(local):
                    first = 2 * local * m + local * c + other
                    pieces.append(recv[phase, band, pl.ds(first, parts, stride=block), :])
                rows.append(jnp.concatenate(pieces, axis=1))
        return jnp.concatenate(rows, axis=0)

    row_id = lax.broadcasted_iota(jnp.int32, (8, n), 0)
    lane_id = lax.broadcasted_iota(jnp.int32, (8, n), 1)

    def lane_sums(value):
        column = jnp.sum(value, axis=0, keepdims=True)
        result = lanes(column, 0)
        for m in range(1, local):
            result = result + lanes(column, m)
        return result

    def send_small(slot, values):
        stacked = jnp.zeros((8, n), f32)
        for i, value in enumerate(values):
            stacked = jnp.where(row_id == i, value, stacked)
        sums = jnp.sum(stacked, axis=1, keepdims=True)
        row = jnp.sum(jnp.where(row_id == lane_id, sums, 0.0), axis=0, keepdims=True)
        small_send[slot] = row
        small_recv[slot, me] = row

        def start(index, _):
            target = peer(index)
            pltpu.make_async_remote_copy(
                src_ref=small_send.at[slot],
                dst_ref=small_recv.at[slot, me],
                send_sem=small_out.at[slot],
                recv_sem=small_in.at[slot],
                device_id={"fft": target},
                device_id_type=MESH,
            ).start()
            return 0

        lax.fori_loop(1, parts, start, 0)

    def receive_small(slot, count):
        wait_bytes(small_recv.at[slot, pl.ds(0, parts - 1)], small_in.at[slot])
        row = jnp.sum(small_recv[slot], axis=0)
        return [
            jnp.sum(jnp.where(lane_id[:1] == i, row, 0.0), axis=1, keepdims=True)
            for i in range(count)
        ]


    def along_z(real, imag, table):
        rows = jnp.concatenate(
            [jnp.concatenate([lanes(real, m), lanes(imag, m)], axis=1) for m in range(local)],
            axis=0,
        )
        out = right_dot(rows, table)
        picked = [out[m * n : (m + 1) * n] for m in range(local)]
        return (
            jnp.concatenate([lanes(v, 0) for v in picked], axis=1),
            jnp.concatenate([lanes(v, 1) for v in picked], axis=1),
        )

    def send_real(phase, band, real, imag):
        real, imag = along_z(real, imag, right[0])
        send_bulk(phase, band, left_dot(left[0], jnp.concatenate([real, imag], axis=0)))

    def receive_real(phase, band):
        out = left_dot(left[1], receive_bulk(phase, band))
        return out[:n], out[n:]

    def send_reciprocal(phase, band, real, imag):
        send_bulk(phase, band, left_dot(left[2], jnp.concatenate([real, imag], axis=0)))

    def receive_reciprocal(phase, band):
        out = left_dot(left[3], receive_bulk(phase, band))
        return along_z(out[:n], out[n:], right[1])


    for band in range(BANDS):
        send_real(0, band, wave[band, 0], wave[band, 1])

    def wavenumber(index):
        signed = jnp.where(2 * index >= n, index - n, index)
        return signed.astype(f32) * unit

    def offset(axis_number):
        bit = lax.rem(pool // 2**axis_number, 2)
        return (0.5 * bit.astype(f32) - 0.25) * unit

    index_x = lax.broadcasted_iota(jnp.int32, (n, n), 0)
    index_z = lax.broadcasted_iota(jnp.int32, (n, n), 1)
    square_x = (wavenumber(index_x) + offset(0)) ** 2
    square_z = (wavenumber(index_z) + offset(2)) ** 2
    for m in range(local):
        square_y = (wavenumber(me * local + m) + offset(1)) ** 2
        value = 0.5 * (square_x + square_y + square_z)
        kin[:, m * n : (m + 1) * n] = value
        pre[:, m * n : (m + 1) * n] = 1.0 / (value + 1.0)

    def wide(ref):
        return jnp.concatenate([ref[m] for m in range(local)], axis=1)


    overlaps = []
    for band in range(BANDS):
        real, imag = receive_real(0, band)
        space_wave[band, 0] = real
        space_wave[band, 1] = imag
        change = wide(perturbation)
        changed_real = change * real
        changed_imag = change * imag
        overlaps.append(lane_sums(changed_real * real + changed_imag * imag))
        if band == BANDS - 1:
            first_real = space_wave[0, 0]
            first_imag = space_wave[0, 1]
            overlaps.append(lane_sums(first_real * changed_real + first_imag * changed_imag))
            overlaps.append(lane_sums(first_real * changed_imag - first_imag * changed_real))
            send_small(0, overlaps)
        send_reciprocal(1, band, changed_real, changed_imag)

    def slot_a(step, band):
        return 1 + BANDS * step + band

    def slot_b(step, band):
        return 1 + BANDS * (CG_STEPS + step) + band

    def search_sums(band, real, imag):
        shifted = kin[...] - energy[0, band]
        sums = [lane_sums(shifted * (real * real + imag * imag))]
        for m in range(BANDS):
            sums.append(lane_sums(wave[m, 0] * real + wave[m, 1] * imag))
            sums.append(lane_sums(wave[m, 0] * imag - wave[m, 1] * real))
        return [value * inverse_total for value in sums]


    partial = [None] * BANDS
    rho = [None] * BANDS
    for band in range(BANDS):
        real, imag = receive_reciprocal(1, band)
        if band == 0:
            same0, same1, cross_real, cross_imag = receive_small(0, 4)
        if band == 0:
            m0_real, m0_imag, m1_real, m1_imag = same0, 0.0 * same0, cross_real, -cross_imag
        else:
            m0_real, m0_imag, m1_real, m1_imag = cross_real, cross_imag, same1, 0.0 * same1
        resid_real = (
            wave[0, 0] * m0_real
            - wave[0, 1] * m0_imag
            + wave[1, 0] * m1_real
            - wave[1, 1] * m1_imag
            - real
        )
        resid_imag = (
            wave[0, 0] * m0_imag
            + wave[0, 1] * m0_real
            + wave[1, 0] * m1_imag
            + wave[1, 1] * m1_real
            - imag
        )
        step_real = pre[...] * resid_real
        step_imag = pre[...] * resid_imag
        send_small(
            slot_a(0, band),
            [lane_sums(resid_real * step_real + resid_imag * step_imag) * inverse_total],
        )
        resid[band, 0] = resid_real
        resid[band, 1] = resid_imag
        search[band, 0] = step_real
        search[band, 1] = step_imag
        send_real(2, band, step_real, step_imag)
    for band in range(BANDS):
        partial[band] = search_sums(band, search[band, 0], search[band, 1])


    step_size = [None] * BANDS
    beta = [None] * BANDS

    def finish_curvature(step, band):
        curvature, c0_real, c0_imag, c1_real, c1_imag = receive_small(slot_b(step, band), 5)
        curvature = curvature + 2.0 * (
            c0_real * c0_real + c0_imag * c0_imag + c1_real * c1_real + c1_imag * c1_imag
        )
        return rho[band] / curvature, c0_real, c0_imag, c1_real, c1_imag

    for step in range(CG_STEPS):
        last = step + 1 == CG_STEPS
        for band in range(BANDS):
            real, imag = receive_real(2 + 2 * step, band)
            if step > 0:
                real = real + beta[band] * space_search[band, 0]
                imag = imag + beta[band] * space_search[band, 1]
            if not last:
                space_search[band, 0] = real
                space_search[band, 1] = imag
            level = wide(potential)
            image_real = level * real
            image_imag = level * imag
            sums = list(partial[band])
            sums[0] = sums[0] + lane_sums(image_real * real + image_imag * imag)
            send_small(slot_b(step, band), sums)
            overlap[band] = space_wave[band, 0] * real + space_wave[band, 1] * imag
            if not last:
                send_reciprocal(3 + 2 * step, band, image_real, image_imag)
        if step == 0:
            for band in range(BANDS):
                (rho[band],) = receive_small(slot_a(0, band), 1)
        if last:
            break
        for band in range(BANDS):
            size, c0_real, c0_imag, c1_real, c1_imag = finish_curvature(step, band)
            added = size * overlap[band]
            if step == 0 and band == 0:
                total[...] = added
            else:
                total[...] = total[...] + added
            pot_real, pot_imag = receive_reciprocal(3 + 2 * step, band)
            shifted = kin[...] - energy[0, band]
            real = search[band, 0]
            imag = search[band, 1]
            image_real = (
                shifted * real
                + pot_real
                + 2.0
                * (
                    wave[0, 0] * c0_real
                    - wave[0, 1] * c0_imag
                    + wave[1, 0] * c1_real
                    - wave[1, 1] * c1_imag
                )
            )
            image_imag = (
                shifted * imag
                + pot_imag
                + 2.0
                * (
                    wave[0, 0] * c0_imag
                    + wave[0, 1] * c0_real
                    + wave[1, 0] * c1_imag
                    + wave[1, 1] * c1_real
                )
            )
            resid_real = resid[band, 0] - size * image_real
            resid_imag = resid[band, 1] - size * image_imag
            step_real = pre[...] * resid_real
            step_imag = pre[...] * resid_imag
            send_small(
                slot_a(step + 1, band),
                [lane_sums(resid_real * step_real + resid_imag * step_imag) * inverse_total],
            )
            resid[band, 0] = resid_real
            resid[band, 1] = resid_imag
            send_real(4 + 2 * step, band, step_real, step_imag)
            step_size[band] = size
        for band in range(BANDS):
            size = step_size[band]
            (rho_new,) = receive_small(slot_a(step + 1, band), 1)
            beta[band] = rho_new / rho[band]
            rho[band] = rho_new
            for c in range(2):
                value = search[band, c]
                moved = size * value
                coeff[band, c] = moved if step == 0 else coeff[band, c] + moved
                search[band, c] = pre[...] * resid[band, c] + beta[band] * value
            partial[band] = search_sums(band, search[band, 0], search[band, 1])


    sums = total[...]
    for band in range(BANDS):
        step_size[band] = finish_curvature(CG_STEPS - 1, band)[0]
        sums = sums + step_size[band] * overlap[band]
    pool_send[...] = exact_dot(y_rows[...], (2.0 * grid_total) * sums).reshape(
        pools, parts, local * n
    )

    def exchange(source, target, which):
        def start(index, _):
            other = pool_peer(index)
            pltpu.make_async_remote_copy(
                src_ref=source.at[other] if which == 0 else source,
                dst_ref=target.at[pool],
                send_sem=pool_out.at[which],
                recv_sem=pool_in.at[which],
                device_id={"pool": other},
                device_id_type=MESH,
            ).start()
            return 0

        lax.fori_loop(1, pools, start, 0)

    def turn(source, target, which):
        here = pl.multiple_of(me * 2 * local, 2 * local)
        target[pl.ds(here, 2 * local), :] = source[pl.ds(here, 2 * local), :]

        def start(index, _):
            other = peer(index)
            there = pl.multiple_of(other * 2 * local, 2 * local)
            pltpu.make_async_remote_copy(
                src_ref=source.at[pl.ds(there, 2 * local)],
                dst_ref=target.at[pl.ds(here, 2 * local)],
                send_sem=turn_out.at[which],
                recv_sem=turn_in.at[which],
                device_id={"fft": other},
                device_id_type=MESH,
            ).start()
            return 0

        lax.fori_loop(1, parts, start, 0)

    def wait_turn(target, which):
        wait_bytes(target.at[pl.ds(0, 2 * local * (parts - 1))], turn_in.at[which])
        return [target[pl.ds(m, parts, stride=2 * local), :] for m in range(local)]

    exchange(pool_send, pool_recv, 0)
    pool_recv[pool] = pool_send[pool]
    go_send[...] = jnp.zeros_like(go_send)
    for band in range(BANDS):
        for c in range(2):
            coeff[band, c] = coeff[band, c] + step_size[band] * search[band, c]
    wait_bytes(pool_recv.at[pl.ds(0, pools - 1)], pool_in.at[0])
    column = jnp.sum(pool_recv[...], axis=0)
    for m in range(local):
        go_send[pl.ds(m, parts, stride=2 * local), :] = lanes(column, m)
    turn(go_send, go_recv, 0)
    own_dens[...] = column
    pool_dens[pool] = column
    exchange(own_dens, pool_dens, 1)


    even = 2 * me
    frequency = jnp.where(
        pool == 0, even, jnp.where(pool == 1, jnp.where(me == 0, n // 2, even), even + 1)
    )

    def plain_square(index):
        k = jnp.where(index > n // 2, index - n // 2, index)
        return (k.astype(f32) * unit) ** 2

    squared = (
        plain_square(index_x) + (frequency.astype(f32) * unit) ** 2 + plain_square(index_z)
    )
    nonzero = (squared > 0).astype(f32)
    coulomb = 4.0 * math.pi * nonzero / (squared + (1.0 - nonzero))

    field = jnp.concatenate(wait_turn(go_recv, 0), axis=0)
    field = exact_dot(exact_dot(x_rows[...], field), z_rows[...])
    field = exact_dot(coulomb * field, z_back[...])
    back_send[...] = exact_dot(x_back[...], field)
    turn(back_send, back_recv, 1)
    wait_bytes(pool_dens.at[pl.ds(0, pools - 1)], pool_in.at[1])
    whole = exact_dot(y_back[...], pool_dens[...].reshape(n, local * n))
    for m in range(local):
        density[m] = lanes(whole, m)
    column = jnp.concatenate(wait_turn(back_recv, 1), axis=1)
    own_hart[...] = column
    pool_hart[pool] = column
    exchange(own_hart, pool_hart, 2)
    wait_bytes(pool_hart.at[pl.ds(0, pools - 1)], pool_in.at[2])
    hartree = exact_dot(y_back[...], pool_hart[...].reshape(n, local * n))
    for m in range(local):
        hxc[m] = lanes(hartree, m) + xc[m] * density[m]


    for phase in range(2 * CG_STEPS + 1):
        for band in range(BANDS):
            wait_bytes(send.at[phase, band, pl.ds(0, parts - 1)], bulk_out.at[phase, band])
    for slot in range(1 + 2 * BANDS * CG_STEPS):
        wait_bytes(small_recv.at[slot, pl.ds(0, parts - 1)], small_out.at[slot])
    for which in range(3):
        wait_bytes(pool_recv.at[pl.ds(0, pools - 1)], pool_out.at[which])
    for which in range(2):
        wait_bytes(go_send.at[pl.ds(0, 2 * local * (parts - 1))], turn_out.at[which])


def body(wave_coeff, band_energy, local_potential, perturbation, xc_kernel, parts, pools):
    n = wave_coeff.shape[-1]
    local = n // parts
    block = 2 * local * local
    wide = local * n
    phases = 2 * CG_STEPS + 1
    slots = 1 + 2 * BANDS * CG_STEPS
    left, right, real = make_tables(n, parts)
    vmem = pl.BlockSpec(memory_space=pltpu.VMEM)
    field = (BANDS, 2, n, wide)
    dma = pltpu.SemaphoreType.DMA
    coeff, density, hxc = pl.pallas_call(
        functools.partial(kernel, n, parts, pools),
        out_shape=(
            jax.ShapeDtypeStruct(field, f32),
            jax.ShapeDtypeStruct((local, n, n), f32),
            jax.ShapeDtypeStruct((local, n, n), f32),
        ),
        in_specs=[vmem, pl.BlockSpec(memory_space=pltpu.SMEM)] + [vmem] * 11,
        out_specs=(vmem, vmem, vmem),
        scratch_shapes=[
            pltpu.VMEM((n, wide), f32),
            pltpu.VMEM((n, wide), f32),
            pltpu.VMEM(field, f32),
            pltpu.VMEM(field, f32),
            pltpu.VMEM(field, f32),
            pltpu.VMEM(field, f32),
            pltpu.VMEM((BANDS, n, wide), f32),
            pltpu.VMEM((n, wide), f32),
            pltpu.VMEM((phases, BANDS, parts, block, n), f32),
            pltpu.VMEM((phases, BANDS, parts * block, n), f32),
            pltpu.VMEM((slots, 1, n), f32),
            pltpu.VMEM((slots, parts, 1, n), f32),
            pltpu.VMEM((pools, parts, wide), f32),
            pltpu.VMEM((pools, parts, wide), f32),
            pltpu.VMEM((pools, parts, wide), f32),
            pltpu.VMEM((pools, parts, wide), f32),
            pltpu.VMEM((parts, wide), f32),
            pltpu.VMEM((parts, wide), f32),
            pltpu.VMEM((2 * n, n), f32),
            pltpu.VMEM((2 * n, n), f32),
            pltpu.VMEM((2 * n, n), f32),
            pltpu.VMEM((2 * n, n), f32),
            dma((phases, BANDS)),
            dma((phases, BANDS)),
            dma((slots,)),
            dma((slots,)),
            dma((3,)),
            dma((3,)),
            dma((2,)),
            dma((2,)),
        ],
        compiler_params=pltpu.CompilerParams(
            collective_id=0, has_side_effects=True, vmem_limit_bytes=56 * 1024 * 1024
        ),
    )(
        wave_coeff.reshape(field),
        band_energy,
        local_potential,
        perturbation,
        xc_kernel,
        jnp.asarray(left),
        jnp.asarray(right),
        *[jnp.asarray(t) for t in real],
    )
    return coeff.reshape(wave_coeff.shape), density, hxc


def solution(mesh):
    return jax.shard_map(
        functools.partial(body, parts=mesh.shape["fft"], pools=mesh.shape["pool"]),
        mesh=mesh,
        in_specs=(
            P("pool", None, None, None, "fft", None),
            P("pool", None),
            P("fft", None, None),
            P("fft", None, None),
            P("fft", None, None),
        ),
        out_specs=(
            P("pool", None, None, None, "fft", None),
            P("fft", None, None),
            P("fft", None, None),
        ),
        check_vma=False,
    )
```

time: 1250 us -> 144 us (0.12)
  blocking collectives: 574 us -> 0 us
  matrix products: 256 us -> 0 us
  waiting for transfers between devices: 156 us -> 0 us
  Pallas kernels: 0 us -> 137 us
  starting transfers between devices: 134 us -> 0 us
  local copies, waits for them, and re-layouts: 95.1 us -> 6.62 us
  between operations: 16.3 us -> 0.66 us
    psum x9 -> x0, blocking collectives: 574 us -> none  [the longest x4 251 us: product_sum(): return lax.psum(local_products(field_real, field_imag), 'fft')]
    dot_general x162 -> x0, matrix products: 256 us -> none  [the longest x130 128 us: contract(): jnp.einsum(pattern, operand, matrix, precision=highest, preferred_element...]
    pallas_call x0 -> x1, Pallas kernels: none -> 137 us  [body(): pl.pallas_call(functools.partial(kernel, n, parts, pools), out_shape=(jax...]
    all_to_all x22 -> x0, starting transfers between devices: 134 us -> none  [the longest x6 43.3 us: to_real(): lax.all_to_all(imag_part, 'fft', split_axis=1, concat_axis=2, tiled=True)]
    all_to_all x22 -> x0, waiting for transfers between devices: 119 us -> none  [the longest x6 39.9 us: to_real(): lax.all_to_all(imag_part, 'fft', split_axis=1, concat_axis=2, tiled=True)]
    psum x1 -> x0, waiting for transfers between devices: 37.2 us -> none  [body(): response_density = lax.psum(density_local, 'pool')]
    add x16 -> x0, local copies, waits for them, and re-layouts: 17 us -> none  [the longest x12 12.4 us: transform(): out_imag = contract(real_part, sine_table) + contract(imag_part, cosine)]
    all_to_all x22 -> x0, local copies, waits for them, and re-layouts: 16.7 us -> none  [the longest x6 4.78 us: to_real(): lax.all_to_all(imag_part, 'fft', split_axis=1, concat_axis=2, tiled=True)]
  transfers between devices with their start and end apart: 23 -> 0, of which waited for: 18 -> 0; matrix products, arithmetic and copies ran while one was open for 16% -> 0% of each run, Pallas kernels for 0% -> 0%
where the time goes in v1:
time: 144 us
  Pallas kernels  137 us (95%)
  local copies, waits for them, and re-layouts  6.62 us (5%)
    pallas_call x1, Pallas kernels, body(): pl.pallas_call(functools.partial(kernel, n, parts, pools), out_shape=(jax...  137 us

profile of v1, /device:TPU:1, one launch (start us, length us, event | category | flops | bytes accessed | tf_op | source)
XLA Modules:
  0.0 144.2 jit_solution(10414227687045002084)
XLA Ops:
  0.6 2.6 %reshape.12.wave = f32[2,2,128,512]{3,2,1,0:T(8,128)} reshape(f32[1,2,2,128,4,128]{5,4,3,2,1,0:T(4,128)} %param.13) | data formatting | bytes 2097152 | tf_op jit(solution)/shard_map/reshape | solution.py:649
  3.2 137.0 %shard_map.148 = (f32[2,2,128,512]{3,2,1,0:T(8,128)}, f32[4,128,128]{2,1,0:T(8,128)}, f32[4,128,128]{2,1,0:T(8,128)}) custom-call(f32[2,2,128,512]{3,2,1,0:T(8,128)} %reshape.12.wave, f32[1,2]{1,0:T(1,128)} %energy.1, f32[4,128,128]{2,1,0:T(8,128)} %potential.1, f32[4,128,128]{2,1,0:T(8,128)} %perturbation.1, f32[4,128,128]{2,1,0:T(8,128)} %xc.1, ...), custom_call_target="tpu_custom_call" | custom-call | tf_op jit(solution)/shard_map/pallas_call | solution.py:604
  140.2 0.0 copy-start.1
  140.2 0.0 copy-start
  140.2 2.6 %reshape.13 = f32[1,2,2,128,4,128]{5,4,3,2,1,0:T(4,128)} reshape(f32[2,2,128,512]{3,2,1,0:T(8,128)} %get-tuple-element.6) | data formatting | bytes 2097152 | tf_op jit(solution)/shard_map/reshape | solution.py:658
  142.8 0.0 copy-done.1
  142.8 0.7 copy.18
  143.5 0.0 copy-done
  143.5 0.7 copy.19
Async XLA Ops:
  140.2 2.6 %copy-start.1 = (f32[4,128,128]{2,1,0:T(8,128)S(1)}, f32[4,128,128]{2,1,0:T(8,128)}, u32[]{:S(2)}) copy-start(f32[4,128,128]{2,1,0:T(8,128)} %get-tuple-element.13) | copy-start | bytes 786436
  140.2 3.3 %copy-start = (f32[4,128,128]{2,1,0:T(8,128)S(1)}, f32[4,128,128]{2,1,0:T(8,128)}, u32[]{:S(2)}) copy-start(f32[4,128,128]{2,1,0:T(8,128)} %get-tuple-element.14) | copy-start | bytes 786436

commit v2 on v1

--- a/solution.py
+++ b/solution.py
@@ -80,12 +80,11 @@
     x_rows = rows[:, by_local_x]
     x_back = np.zeros((parts, 2 * local, n))
     x_back[:, :local] = back.T.reshape(parts, local, n)
-    real = [y_rows, y_back.T, x_rows, x_back.reshape(2 * n, n), rows.T, back]
-    return left, right, [np.asarray(t, np.float32) for t in real]
-
-
-def exact_dot(a, b):
-    return jnp.dot(a, b, precision=lax.Precision.HIGHEST, preferred_element_type=f32)
+    basis_y = np.stack([split_table(y_rows * 2.0 * n**3, 1), split_table(y_back.T, 1)])
+    basis_z = np.stack([split_table(rows.T, 0), split_table(back, 0)])
+    basis_x = split_table(x_rows, 1)
+    spread_x = split_table(x_back.reshape(2 * n, n), 1)
+    return [left, right, basis_y, basis_x, spread_x, basis_z]
 
 
 def halves(value):
@@ -108,26 +107,37 @@
     n,
     parts,
     pools,
-    wave,
+    grid,
+    raw_hbm,
     energy,
+    potential_hbm,
+    perturbation_hbm,
+    xc_hbm,
+    left_hbm,
+    right_hbm,
+    basis_y_hbm,
+    basis_x_hbm,
+    spread_x_hbm,
+    basis_z_hbm,
+    coeff,
+    density,
+    hxc,
+    raw,
     potential,
     perturbation,
     xc,
     left,
     right,
-    y_rows,
-    y_back,
-    x_rows,
-    x_back,
-    z_rows,
-    z_back,
-    coeff,
-    density,
-    hxc,
+    basis_y,
+    basis_x,
+    spread_x,
+    basis_z,
+    wave,
     kin,
     pre,
     resid,
     search,
+    answer,
     space_wave,
     space_search,
     overlap,
@@ -136,79 +146,107 @@
     recv,
     small_send,
     small_recv,
-    pool_send,
-    pool_recv,
-    pool_dens,
-    pool_hart,
-    own_dens,
-    own_hart,
     go_send,
     go_recv,
     back_send,
     back_recv,
+    loaded,
     bulk_out,
     bulk_in,
     small_out,
     small_in,
-    pool_out,
-    pool_in,
     turn_out,
     turn_in,
 ):
     local = n // parts
     block = 2 * local * local
-    grid_total = n**3
-    inverse_total = 1.0 / grid_total
+    devices = parts * pools
+    inverse_total = 1.0 / n**3
     me = lax.axis_index("fft")
     pool = lax.axis_index("pool")
+    size_z, size_x, size_c = grid
+    my_z, my_x, my_c = me // (size_x * size_c), lax.rem(me // size_c, size_x), lax.rem(me, size_c)
+    at_self = (-(size_z // 2) % size_z) * size_x * size_c + (-(size_x // 2) % size_x) * size_c
 
     def lanes(value, index):
         return value[:, index * n : (index + 1) * n]
 
     def peer(index):
-        return lax.rem(me + index, parts)
-
-    def pool_peer(index):
-        return lax.rem(pool + index, pools)
+        z = lax.rem(my_z + size_z // 2 + index // (size_x * size_c), size_z)
+        x = lax.rem(my_x + size_x // 2 + lax.rem(index // size_c, size_x), size_x)
+        c = lax.rem(my_c + lax.rem(index, size_c), size_c)
+        return (z * size_x + x) * size_c + c
+
+    def for_peers(act):
+        def step(index, _):
+            act(peer(index))
+            return 0
+
+        lax.fori_loop(0, at_self, step, 0)
+        lax.fori_loop(at_self + 1, parts, step, 0)
+
+    def for_devices(act):
+        for shift in (2, 1, 3):
+            other_pool = lax.rem(pool + shift, pools)
+
+            def step(index, _, other_pool=other_pool):
+                act(peer(index), other_pool)
+                return 0
+
+            lax.fori_loop(0, parts, step, 0)
+        for_peers(lambda other: act(other, pool))
 
     barrier = pltpu.get_barrier_semaphore()
 
-    def greet(index, _):
-        pl.semaphore_signal(barrier, inc=1, device_id={"fft": peer(index)}, device_id_type=MESH)
-        return 0
-
-    def greet_pool(index, _):
+    def greet(other, other_pool):
         pl.semaphore_signal(
-            barrier, inc=1, device_id={"pool": pool_peer(index)}, device_id_type=MESH
+            barrier, inc=1, device_id={"pool": other_pool, "fft": other}, device_id_type=MESH
         )
-        return 0
-
-    lax.fori_loop(1, parts, greet, 0)
-    lax.fori_loop(1, pools, greet_pool, 0)
-    pl.semaphore_wait(barrier, parts + pools - 2)
-
-
-    def send_bulk(phase, band, value):
+
+    for_devices(greet)
+    loads = {}
+    order = [
+        (raw_hbm, raw),
+        (right_hbm, right),
+        (left_hbm, left),
+        (perturbation_hbm, perturbation),
+        (potential_hbm, potential),
+        (basis_y_hbm, basis_y),
+        (basis_x_hbm, basis_x),
+        (basis_z_hbm, basis_z),
+        (spread_x_hbm, spread_x),
+        (xc_hbm, xc),
+    ]
+    for i, (source, target) in enumerate(order):
+        loads[i] = pltpu.make_async_copy(source, target, loaded.at[i])
+        loads[i].start()
+
+
+    def store_bulk(phase, band, value):
         for m in range(local):
             send[phase, band, :, 2 * local * m : 2 * local * (m + 1), :] = lanes(value, m).reshape(
                 parts, 2 * local, n
             )
+
+    def start_bulk(phase, band):
         here = pl.multiple_of(me * block, block)
-        recv[phase, band, pl.ds(here, block), :] = send[phase, band, me]
-
-        def start(index, _):
-            target = peer(index)
+
+        def start(other):
             pltpu.make_async_remote_copy(
-                src_ref=send.at[phase, band, target],
+                src_ref=send.at[phase, band, other],
                 dst_ref=recv.at[phase, band, pl.ds(here, block)],
                 send_sem=bulk_out.at[phase, band],
                 recv_sem=bulk_in.at[phase, band],
-                device_id={"fft": target},
+                device_id={"fft": other},
                 device_id_type=MESH,
             ).start()
-            return 0
-
-        lax.fori_loop(1, parts, start, 0)
+
+        for_peers(start)
+        recv[phase, band, pl.ds(here, block), :] = send[phase, band, me]
+
+    def send_bulk(phase, band, value):
+        store_bulk(phase, band, value)
+        start_bulk(phase, band)
 
     def wait_bytes(ref, sem):
         pltpu.make_async_copy(ref, ref, sem).wait()
@@ -244,19 +282,17 @@
         small_send[slot] = row
         small_recv[slot, me] = row
 
-        def start(index, _):
-            target = peer(index)
+        def start(other):
             pltpu.make_async_remote_copy(
                 src_ref=small_send.at[slot],
                 dst_ref=small_recv.at[slot, me],
                 send_sem=small_out.at[slot],
                 recv_sem=small_in.at[slot],
-                device_id={"fft": target},
+                device_id={"fft": other},
                 device_id_type=MESH,
             ).start()
-            return 0
-
-        lax.fori_loop(1, parts, start, 0)
+
+        for_peers(start)
 
     def receive_small(slot, count):
         wait_bytes(small_recv.at[slot, pl.ds(0, parts - 1)], small_in.at[slot])
@@ -295,8 +331,21 @@
         return along_z(out[:n], out[n:], right[1])
 
 
+    loads[0].wait()
     for band in range(BANDS):
-        send_real(0, band, wave[band, 0], wave[band, 1])
+        for c in range(2):
+            for m in range(local):
+                wave[band, c, :, m * n : (m + 1) * n] = raw[
+                    band, c, pl.ds(m, n, stride=local), :
+                ]
+        if band == 0:
+            loads[1].wait()
+            loads[2].wait()
+        real, imag = along_z(wave[band, 0], wave[band, 1], right[0])
+        store_bulk(0, band, left_dot(left[0], jnp.concatenate([real, imag], axis=0)))
+        if band == 0:
+            pl.semaphore_wait(barrier, devices - 1)
+        start_bulk(0, band)
 
     def wavenumber(index):
         signed = jnp.where(2 * index >= n, index - n, index)
@@ -321,6 +370,8 @@
 
 
     overlaps = []
+    for i in range(3, len(order)):
+        loads[i].wait()
     for band in range(BANDS):
         real, imag = receive_real(0, band)
         space_wave[band, 0] = real
@@ -387,8 +438,6 @@
         search[band, 0] = step_real
         search[band, 1] = step_imag
         send_real(2, band, step_real, step_imag)
-    for band in range(BANDS):
-        partial[band] = search_sums(band, search[band, 0], search[band, 1])
 
 
     step_size = [None] * BANDS
@@ -401,9 +450,23 @@
         )
         return rho[band] / curvature, c0_real, c0_imag, c1_real, c1_imag
 
+    def next_search(step, band):
+        size = step_size[band]
+        (rho_new,) = receive_small(slot_a(step, band), 1)
+        beta[band] = rho_new / rho[band]
+        rho[band] = rho_new
+        for c in range(2):
+            value = search[band, c]
+            moved = size * value
+            answer[band, c] = moved if step == 1 else answer[band, c] + moved
+            search[band, c] = pre[...] * resid[band, c] + beta[band] * value
+
     for step in range(CG_STEPS):
         last = step + 1 == CG_STEPS
         for band in range(BANDS):
+            if step > 0:
+                next_search(step, band)
+            partial[band] = search_sums(band, search[band, 0], search[band, 1])
             real, imag = receive_real(2 + 2 * step, band)
             if step > 0:
                 real = real + beta[band] * space_search[band, 0]
@@ -470,80 +533,45 @@
             resid[band, 1] = resid_imag
             send_real(4 + 2 * step, band, step_real, step_imag)
             step_size[band] = size
-        for band in range(BANDS):
-            size = step_size[band]
-            (rho_new,) = receive_small(slot_a(step + 1, band), 1)
-            beta[band] = rho_new / rho[band]
-            rho[band] = rho_new
-            for c in range(2):
-                value = search[band, c]
-                moved = size * value
-                coeff[band, c] = moved if step == 0 else coeff[band, c] + moved
-                search[band, c] = pre[...] * resid[band, c] + beta[band] * value
-            partial[band] = search_sums(band, search[band, 0], search[band, 1])
-
-
-    sums = total[...]
+
+    columns = left_dot(basis_y[0], total[...])
+    moved = [left_dot(basis_y[0], overlap[band]) for band in range(BANDS)]
     for band in range(BANDS):
         step_size[band] = finish_curvature(CG_STEPS - 1, band)[0]
-        sums = sums + step_size[band] * overlap[band]
-    pool_send[...] = exact_dot(y_rows[...], (2.0 * grid_total) * sums).reshape(
-        pools, parts, local * n
-    )
-
-    def exchange(source, target, which):
-        def start(index, _):
-            other = pool_peer(index)
+        columns = columns + step_size[band] * moved[band]
+
+    slot = 2 * local
+
+    def turn(which, source, target, all_columns):
+        here = pl.multiple_of((pool * parts + me) * slot, slot)
+        own = here if all_columns else pl.multiple_of(me * slot, slot)
+        target[pl.ds(here, local), :] = source[pl.ds(own, local), :]
+
+        def start(other, other_pool):
+            there = other_pool * parts + other if all_columns else other
+            there = pl.multiple_of(there * slot, slot)
             pltpu.make_async_remote_copy(
-                src_ref=source.at[other] if which == 0 else source,
-                dst_ref=target.at[pool],
-                send_sem=pool_out.at[which],
-                recv_sem=pool_in.at[which],
-                device_id={"pool": other},
+                src_ref=source.at[pl.ds(there, local)],
+                dst_ref=target.at[pl.ds(here, local)],
+                send_sem=turn_out.at[which],
+                recv_sem=turn_in.at[which],
+                device_id={"pool": other_pool, "fft": other},
                 device_id_type=MESH,
             ).start()
-            return 0
-
-        lax.fori_loop(1, pools, start, 0)
-
-    def turn(source, target, which):
-        here = pl.multiple_of(me * 2 * local, 2 * local)
-        target[pl.ds(here, 2 * local), :] = source[pl.ds(here, 2 * local), :]
-
-        def start(index, _):
-            other = peer(index)
-            there = pl.multiple_of(other * 2 * local, 2 * local)
-            pltpu.make_async_remote_copy(
-                src_ref=source.at[pl.ds(there, 2 * local)],
-                dst_ref=target.at[pl.ds(here, 2 * local)],
-                send_sem=turn_out.at[which],
-                recv_sem=turn_in.at[which],
-                device_id={"fft": other},
-                device_id_type=MESH,
-            ).start()
-            return 0
-
-        lax.fori_loop(1, parts, start, 0)
-
-    def wait_turn(target, which):
-        wait_bytes(target.at[pl.ds(0, 2 * local * (parts - 1))], turn_in.at[which])
-        return [target[pl.ds(m, parts, stride=2 * local), :] for m in range(local)]
-
-    exchange(pool_send, pool_recv, 0)
-    pool_recv[pool] = pool_send[pool]
-    go_send[...] = jnp.zeros_like(go_send)
+
+        for_devices(start)
+
+    def wait_turn(which, target):
+        wait_bytes(target.at[pl.ds(0, local * (devices - 1))], turn_in.at[which])
+
+    for m in range(local):
+        go_send[pl.ds(m, devices, stride=slot), :] = lanes(columns, m)
+    turn(0, go_send, go_recv, True)
     for band in range(BANDS):
         for c in range(2):
-            coeff[band, c] = coeff[band, c] + step_size[band] * search[band, c]
-    wait_bytes(pool_recv.at[pl.ds(0, pools - 1)], pool_in.at[0])
-    column = jnp.sum(pool_recv[...], axis=0)
-    for m in range(local):
-        go_send[pl.ds(m, parts, stride=2 * local), :] = lanes(column, m)
-    turn(go_send, go_recv, 0)
-    own_dens[...] = column
-    pool_dens[pool] = column
-    exchange(own_dens, pool_dens, 1)
-
+            value = answer[band, c] + step_size[band] * search[band, c]
+            for m in range(local):
+                coeff[band, c, pl.ds(m, n, stride=local), :] = lanes(value, m)
 
     even = 2 * me
     frequency = jnp.where(
@@ -560,23 +588,32 @@
     nonzero = (squared > 0).astype(f32)
     coulomb = 4.0 * math.pi * nonzero / (squared + (1.0 - nonzero))
 
-    field = jnp.concatenate(wait_turn(go_recv, 0), axis=0)
-    field = exact_dot(exact_dot(x_rows[...], field), z_rows[...])
-    field = exact_dot(coulomb * field, z_back[...])
-    back_send[...] = exact_dot(x_back[...], field)
-    turn(back_send, back_recv, 1)
-    wait_bytes(pool_dens.at[pl.ds(0, pools - 1)], pool_in.at[1])
-    whole = exact_dot(y_back[...], pool_dens[...].reshape(n, local * n))
+    wait_turn(0, go_recv)
+    pieces = []
     for m in range(local):
-        density[m] = lanes(whole, m)
-    column = jnp.concatenate(wait_turn(back_recv, 1), axis=1)
-    own_hart[...] = column
-    pool_hart[pool] = column
-    exchange(own_hart, pool_hart, 2)
-    wait_bytes(pool_hart.at[pl.ds(0, pools - 1)], pool_in.at[2])
-    hartree = exact_dot(y_back[...], pool_hart[...].reshape(n, local * n))
-    for m in range(local):
-        hxc[m] = lanes(hartree, m) + xc[m] * density[m]
+        piece = go_recv[pl.ds(m, parts, stride=slot), :]
+        for other in range(1, pools):
+            piece = piece + go_recv[pl.ds(other * parts * slot + m, parts, stride=slot), :]
+        back_send[0, pl.ds(m, parts, stride=slot), :] = piece
+        pieces.append(piece)
+    turn(1, back_send.at[0], back_recv.at[0], False)
+
+
+    field = left_dot(basis_x[...], jnp.concatenate(pieces, axis=0))
+    field = coulomb * right_dot(field, basis_z[0])
+    field = left_dot(spread_x[...], right_dot(field, basis_z[1]))
+    back_send[1] = field
+    turn(2, back_send.at[1], back_recv.at[1], False)
+
+    for i, result in enumerate((density, hxc)):
+        wait_turn(1 + i, back_recv.at[i])
+        columns = [back_recv[i, pl.ds(m, devices, stride=slot), :] for m in range(local)]
+        whole = left_dot(basis_y[1], jnp.concatenate(columns, axis=1))
+        for m in range(local):
+            if i == 0:
+                result[m] = lanes(whole, m)
+            else:
+                result[m] = lanes(whole, m) + xc[m] * density[m]
 
 
     for phase in range(2 * CG_STEPS + 1):
@@ -585,9 +622,7 @@
     for slot in range(1 + 2 * BANDS * CG_STEPS):
         wait_bytes(small_recv.at[slot, pl.ds(0, parts - 1)], small_out.at[slot])
     for which in range(3):
-        wait_bytes(pool_recv.at[pl.ds(0, pools - 1)], pool_out.at[which])
-    for which in range(2):
-        wait_bytes(go_send.at[pl.ds(0, 2 * local * (parts - 1))], turn_out.at[which])
+        wait_bytes(go_recv.at[pl.ds(0, local * (devices - 1))], turn_out.at[which])
 
 
 def body(wave_coeff, band_energy, local_potential, perturbation, xc_kernel, parts, pools):
@@ -597,64 +632,59 @@
     wide = local * n
     phases = 2 * CG_STEPS + 1
     slots = 1 + 2 * BANDS * CG_STEPS
-    left, right, real = make_tables(n, parts)
+    slot_rows = 2 * local * parts
+    grid = (4, 4, 2) if parts == 32 else (1, parts, 1)
+    operands = [
+        wave_coeff.reshape(BANDS, 2, n * local, n),
+        local_potential,
+        perturbation,
+        xc_kernel,
+    ] + [jnp.asarray(t) for t in make_tables(n, parts)]
+    anywhere = pl.BlockSpec(memory_space=pl.ANY)
     vmem = pl.BlockSpec(memory_space=pltpu.VMEM)
-    field = (BANDS, 2, n, wide)
+    field = pltpu.VMEM((BANDS, 2, n, wide), f32)
     dma = pltpu.SemaphoreType.DMA
     coeff, density, hxc = pl.pallas_call(
-        functools.partial(kernel, n, parts, pools),
+        functools.partial(kernel, n, parts, pools, grid),
         out_shape=(
-            jax.ShapeDtypeStruct(field, f32),
+            jax.ShapeDtypeStruct(operands[0].shape, f32),
             jax.ShapeDtypeStruct((local, n, n), f32),
             jax.ShapeDtypeStruct((local, n, n), f32),
         ),
-        in_specs=[vmem, pl.BlockSpec(memory_space=pltpu.SMEM)] + [vmem] * 11,
+        in_specs=[anywhere, pl.BlockSpec(memory_space=pltpu.SMEM)] + [anywhere] * 9,
         out_specs=(vmem, vmem, vmem),
-        scratch_shapes=[
+        scratch_shapes=[pltpu.VMEM(t.shape, t.dtype) for t in operands]
+        + [
+            field,
             pltpu.VMEM((n, wide), f32),
             pltpu.VMEM((n, wide), f32),
-            pltpu.VMEM(field, f32),
-            pltpu.VMEM(field, f32),
-            pltpu.VMEM(field, f32),
-            pltpu.VMEM(field, f32),
+            field,
+            field,
+            field,
+            field,
+            field,
             pltpu.VMEM((BANDS, n, wide), f32),
             pltpu.VMEM((n, wide), f32),
             pltpu.VMEM((phases, BANDS, parts, block, n), f32),
             pltpu.VMEM((phases, BANDS, parts * block, n), f32),
             pltpu.VMEM((slots, 1, n), f32),
             pltpu.VMEM((slots, parts, 1, n), f32),
-            pltpu.VMEM((pools, parts, wide), f32),
-            pltpu.VMEM((pools, parts, wide), f32),
-            pltpu.VMEM((pools, parts, wide), f32),
-            pltpu.VMEM((pools, parts, wide), f32),
-            pltpu.VMEM((parts, wide), f32),
-            pltpu.VMEM((parts, wide), f32),
-            pltpu.VMEM((2 * n, n), f32),
-            pltpu.VMEM((2 * n, n), f32),
-            pltpu.VMEM((2 * n, n), f32),
-            pltpu.VMEM((2 * n, n), f32),
+            pltpu.VMEM((pools * slot_rows, n), f32),
+            pltpu.VMEM((pools * slot_rows, n), f32),
+            pltpu.VMEM((2, slot_rows, n), f32),
+            pltpu.VMEM((2, pools * slot_rows, n), f32),
+            dma((10,)),
             dma((phases, BANDS)),
             dma((phases, BANDS)),
             dma((slots,)),
             dma((slots,)),
             dma((3,)),
             dma((3,)),
-            dma((2,)),
-            dma((2,)),
         ],
         compiler_params=pltpu.CompilerParams(
             collective_id=0, has_side_effects=True, vmem_limit_bytes=56 * 1024 * 1024
         ),
-    )(
-        wave_coeff.reshape(field),
-        band_energy,
-        local_potential,
-        perturbation,
-        xc_kernel,
-        jnp.asarray(left),
-        jnp.asarray(right),
-        *[jnp.asarray(t) for t in real],
-    )
+    )(operands[0], band_energy, *operands[1:])
     return coeff.reshape(wave_coeff.shape), density, hxc
 
 

time: 144 us -> 138 us (0.958)
  Pallas kernels: 137 us -> 133 us
  local copies, waits for them, and re-layouts: 6.62 us -> 3.73 us
    reshape x2 -> x0, local copies, waits for them, and re-layouts: 5.2 us -> none  [the longest x1 2.61 us: body(): wave_coeff.reshape(field)]
    pallas_call x1, Pallas kernels: 137 us -> 133 us  [body(): pl.pallas_call(functools.partial(kernel, n, parts, pools, grid), out_shap...]
    unnamed x6 -> x7, local copies, waits for them, and re-layouts: 1.41 us -> 3.73 us
where the time goes in v2:
time: 138 us
  Pallas kernels  133 us (96%)
  local copies, waits for them, and re-layouts  3.73 us (3%)
    pallas_call x1, Pallas kernels, body(): pl.pallas_call(functools.partial(kernel, n, parts, pools, grid), out_shap...  133 us
    unnamed x7, local copies, waits for them, and re-layouts  3.73 us

profile of v2, /device:TPU:1, one launch (start us, length us, event | category | flops | bytes accessed | tf_op | source)
XLA Modules:
  0.0 137.8 jit_solution(17455528954963845221)
XLA Ops:
  0.6 133.4 %shard_map.130 = (f32[2,2,512,128]{3,2,1,0:T(8,128)}, f32[4,128,128]{2,1,0:T(8,128)}, f32[4,128,128]{2,1,0:T(8,128)}) custom-call(f32[2,2,512,128]{3,2,1,0:T(8,128)} %bitcast.2, f32[1,2]{1,0:T(1,128)} %energy.1, f32[4,128,128]{2,1,0:T(8,128)} %potential_hbm.1, f32[4,128,128]{2,1,0:T(8,128)} %perturbation_hbm.1, f32[4,128,128]{2,1,0:T(8,128)} %xc_hbm.1, ...), custom_call_target="tpu_custom_call" | custom-call | tf_op jit(solution)/shard_map/pallas_call | solution.py:647
  134.0 0.0 copy-start.1
  134.0 0.0 copy-start
  134.0 2.3 %copy.17 = f32[1,2,2,128,4,128]{5,4,3,2,1,0:T(4,128)} copy(f32[1,2,2,128,4,128]{5,4,3,2,1,0:T(4,128)} %bitcast.3) | data formatting | bytes 2097152
  136.3 0.0 copy-done.1
  136.3 0.7 copy.18
  137.1 0.0 copy-done
  137.1 0.7 copy.19
Async XLA Ops:
  134.0 2.3 %copy-start.1 = (f32[4,128,128]{2,1,0:T(8,128)S(1)}, f32[4,128,128]{2,1,0:T(8,128)}, u32[]{:S(2)}) copy-start(f32[4,128,128]{2,1,0:T(8,128)} %get-tuple-element.13) | copy-start | bytes 786436
  134.0 3.0 %copy-start = (f32[4,128,128]{2,1,0:T(8,128)S(1)}, f32[4,128,128]{2,1,0:T(8,128)}, u32[]{:S(2)}) copy-start(f32[4,128,128]{2,1,0:T(8,128)} %get-tuple-element.14) | copy-start | bytes 786436

commit v3 on v2

--- a/solution.py
+++ b/solution.py
@@ -138,6 +138,7 @@
     resid,
     search,
     answer,
+    ahead,
     space_wave,
     space_search,
     overlap,
@@ -160,6 +161,7 @@
 ):
     local = n // parts
     block = 2 * local * local
+    room = block + 8
     devices = parts * pools
     inverse_total = 1.0 / n**3
     me = lax.axis_index("fft")
@@ -228,13 +230,16 @@
                 parts, 2 * local, n
             )
 
-    def start_bulk(phase, band):
-        here = pl.multiple_of(me * block, block)
+    def start_bulk(phase, band, row=None):
+        here = pl.multiple_of(me * room, room)
+        used = block if row is None else block + 1
+        if row is not None:
+            send[phase, band, :, block : block + 8, :] = jnp.broadcast_to(row, (parts, 8, n))
 
         def start(other):
             pltpu.make_async_remote_copy(
-                src_ref=send.at[phase, band, other],
-                dst_ref=recv.at[phase, band, pl.ds(here, block)],
+                src_ref=send.at[phase, band, other, pl.ds(0, used)],
+                dst_ref=recv.at[phase, band, pl.ds(here, used)],
                 send_sem=bulk_out.at[phase, band],
                 recv_sem=bulk_in.at[phase, band],
                 device_id={"fft": other},
@@ -242,24 +247,27 @@
             ).start()
 
         for_peers(start)
-        recv[phase, band, pl.ds(here, block), :] = send[phase, band, me]
-
-    def send_bulk(phase, band, value):
+        recv[phase, band, pl.ds(here, room), :] = send[phase, band, me]
+
+    def send_bulk(phase, band, value, row=None):
         store_bulk(phase, band, value)
-        start_bulk(phase, band)
+        start_bulk(phase, band, row)
+
+    def bulk_rows(phase):
+        return (parts - 1) * (block + 1 if phase >= 2 else block)
 
     def wait_bytes(ref, sem):
         pltpu.make_async_copy(ref, ref, sem).wait()
 
     def receive_bulk(phase, band):
-        wait_bytes(recv.at[phase, band, pl.ds(0, block * (parts - 1))], bulk_in.at[phase, band])
+        wait_bytes(recv.at[phase, band, pl.ds(0, bulk_rows(phase))], bulk_in.at[phase, band])
         rows = []
         for c in range(2):
             for m in range(local):
                 pieces = []
                 for other in range(local):
                     first = 2 * local * m + local * c + other
-                    pieces.append(recv[phase, band, pl.ds(first, parts, stride=block), :])
+                    pieces.append(recv[phase, band, pl.ds(first, parts, stride=room), :])
                 rows.append(jnp.concatenate(pieces, axis=1))
         return jnp.concatenate(rows, axis=0)
 
@@ -273,12 +281,25 @@
             result = result + lanes(column, m)
         return result
 
-    def send_small(slot, values):
+    def pack(values):
         stacked = jnp.zeros((8, n), f32)
         for i, value in enumerate(values):
             stacked = jnp.where(row_id == i, value, stacked)
         sums = jnp.sum(stacked, axis=1, keepdims=True)
-        row = jnp.sum(jnp.where(row_id == lane_id, sums, 0.0), axis=0, keepdims=True)
+        return jnp.sum(jnp.where(row_id == lane_id, sums, 0.0), axis=0, keepdims=True)
+
+    def unpack(row, count):
+        return [
+            jnp.sum(jnp.where(lane_id[:1] == i, row, 0.0), axis=1, keepdims=True)
+            for i in range(count)
+        ]
+
+    def bulk_row(phase, band, count):
+        rows = recv[phase, band, pl.ds(block, parts, stride=room), :]
+        return unpack(jnp.sum(rows, axis=0, keepdims=True), count)
+
+    def send_small(slot, values):
+        row = pack(values)
         small_send[slot] = row
         small_recv[slot, me] = row
 
@@ -296,11 +317,7 @@
 
     def receive_small(slot, count):
         wait_bytes(small_recv.at[slot, pl.ds(0, parts - 1)], small_in.at[slot])
-        row = jnp.sum(small_recv[slot], axis=0)
-        return [
-            jnp.sum(jnp.where(lane_id[:1] == i, row, 0.0), axis=1, keepdims=True)
-            for i in range(count)
-        ]
+        return unpack(jnp.sum(small_recv[slot], axis=0), count)
 
 
     def along_z(real, imag, table):
@@ -315,16 +332,16 @@
             jnp.concatenate([lanes(v, 1) for v in picked], axis=1),
         )
 
-    def send_real(phase, band, real, imag):
+    def send_real(phase, band, real, imag, row):
         real, imag = along_z(real, imag, right[0])
-        send_bulk(phase, band, left_dot(left[0], jnp.concatenate([real, imag], axis=0)))
+        send_bulk(phase, band, left_dot(left[0], jnp.concatenate([real, imag], axis=0)), row)
 
     def receive_real(phase, band):
         out = left_dot(left[1], receive_bulk(phase, band))
         return out[:n], out[n:]
 
-    def send_reciprocal(phase, band, real, imag):
-        send_bulk(phase, band, left_dot(left[2], jnp.concatenate([real, imag], axis=0)))
+    def send_reciprocal(phase, band, real, imag, row=None):
+        send_bulk(phase, band, left_dot(left[2], jnp.concatenate([real, imag], axis=0)), row)
 
     def receive_reciprocal(phase, band):
         out = left_dot(left[3], receive_bulk(phase, band))
@@ -388,19 +405,26 @@
             send_small(0, overlaps)
         send_reciprocal(1, band, changed_real, changed_imag)
 
-    def slot_a(step, band):
-        return 1 + BANDS * step + band
-
-    def slot_b(step, band):
-        return 1 + BANDS * (CG_STEPS + step) + band
-
-    def search_sums(band, real, imag):
-        shifted = kin[...] - energy[0, band]
-        sums = [lane_sums(shifted * (real * real + imag * imag))]
+    def products(band, real, imag):
+        sums = []
         for m in range(BANDS):
             sums.append(lane_sums(wave[m, 0] * real + wave[m, 1] * imag))
             sums.append(lane_sums(wave[m, 0] * imag - wave[m, 1] * real))
         return [value * inverse_total for value in sums]
+
+    def kinetic_sum(band, left_real, left_imag, right_real, right_imag):
+        shifted = kin[...] - energy[0, band]
+        return lane_sums(shifted * (left_real * right_real + left_imag * right_imag)) * inverse_total
+
+    def send_step(phase, band, resid_real, resid_imag):
+        real = pre[...] * resid_real
+        imag = pre[...] * resid_imag
+        row = pack([lane_sums(resid_real * real + resid_imag * imag) * inverse_total])
+        resid[band, 0] = resid_real
+        resid[band, 1] = resid_imag
+        ahead[band, 0] = real
+        ahead[band, 1] = imag
+        send_real(phase, band, real, imag, row)
 
 
     partial = [None] * BANDS
@@ -427,75 +451,61 @@
             + wave[1, 1] * m1_real
             - imag
         )
-        step_real = pre[...] * resid_real
-        step_imag = pre[...] * resid_imag
-        send_small(
-            slot_a(0, band),
-            [lane_sums(resid_real * step_real + resid_imag * step_imag) * inverse_total],
-        )
-        resid[band, 0] = resid_real
-        resid[band, 1] = resid_imag
-        search[band, 0] = step_real
-        search[band, 1] = step_imag
-        send_real(2, band, step_real, step_imag)
+        send_step(2, band, resid_real, resid_imag)
 
 
     step_size = [None] * BANDS
-    beta = [None] * BANDS
-
-    def finish_curvature(step, band):
-        curvature, c0_real, c0_imag, c1_real, c1_imag = receive_small(slot_b(step, band), 5)
+
+    def finish_curvature(band, values):
+        curvature, c0_real, c0_imag, c1_real, c1_imag = values
         curvature = curvature + 2.0 * (
             c0_real * c0_real + c0_imag * c0_imag + c1_real * c1_real + c1_imag * c1_imag
         )
-        return rho[band] / curvature, c0_real, c0_imag, c1_real, c1_imag
-
-    def next_search(step, band):
-        size = step_size[band]
-        (rho_new,) = receive_small(slot_a(step, band), 1)
-        beta[band] = rho_new / rho[band]
-        rho[band] = rho_new
-        for c in range(2):
-            value = search[band, c]
-            moved = size * value
-            answer[band, c] = moved if step == 1 else answer[band, c] + moved
-            search[band, c] = pre[...] * resid[band, c] + beta[band] * value
+        return rho[band] / curvature
 
     for step in range(CG_STEPS):
         last = step + 1 == CG_STEPS
         for band in range(BANDS):
+            real, imag = ahead[band, 0], ahead[band, 1]
+            sums = [kinetic_sum(band, real, imag, real, imag)] + products(band, real, imag)
             if step > 0:
-                next_search(step, band)
-            partial[band] = search_sums(band, search[band, 0], search[band, 1])
+                cross = kinetic_sum(band, real, imag, search[band, 0], search[band, 1])
             real, imag = receive_real(2 + 2 * step, band)
+            (rho_new,) = bulk_row(2 + 2 * step, band, 1)
             if step > 0:
-                real = real + beta[band] * space_search[band, 0]
-                imag = imag + beta[band] * space_search[band, 1]
+                beta = rho_new / rho[band]
+                before = partial[band]
+                sums[0] = sums[0] + beta * (2.0 * cross + beta * before[0])
+                for i in range(1, 1 + 2 * BANDS):
+                    sums[i] = sums[i] + beta * before[i]
+                real = real + beta * space_search[band, 0]
+                imag = imag + beta * space_search[band, 1]
+            rho[band] = rho_new
+            partial[band] = list(sums)
             if not last:
                 space_search[band, 0] = real
                 space_search[band, 1] = imag
             level = wide(potential)
             image_real = level * real
             image_imag = level * imag
-            sums = list(partial[band])
             sums[0] = sums[0] + lane_sums(image_real * real + image_imag * imag)
-            send_small(slot_b(step, band), sums)
+            if last:
+                send_small(1 + band, sums)
+            else:
+                send_reciprocal(3 + 2 * step, band, image_real, image_imag, pack(sums))
             overlap[band] = space_wave[band, 0] * real + space_wave[band, 1] * imag
-            if not last:
-                send_reciprocal(3 + 2 * step, band, image_real, image_imag)
-        if step == 0:
-            for band in range(BANDS):
-                (rho[band],) = receive_small(slot_a(0, band), 1)
+            for c in range(2):
+                if step == 0:
+                    search[band, c] = ahead[band, c]
+                else:
+                    search[band, c] = ahead[band, c] + beta * search[band, c]
         if last:
             break
         for band in range(BANDS):
-            size, c0_real, c0_imag, c1_real, c1_imag = finish_curvature(step, band)
-            added = size * overlap[band]
-            if step == 0 and band == 0:
-                total[...] = added
-            else:
-                total[...] = total[...] + added
             pot_real, pot_imag = receive_reciprocal(3 + 2 * step, band)
+            values = bulk_row(3 + 2 * step, band, 5)
+            _, c0_real, c0_imag, c1_real, c1_imag = values
+            size = finish_curvature(band, values)
             shifted = kin[...] - energy[0, band]
             real = search[band, 0]
             imag = search[band, 1]
@@ -521,23 +531,23 @@
                     + wave[1, 1] * c1_real
                 )
             )
-            resid_real = resid[band, 0] - size * image_real
-            resid_imag = resid[band, 1] - size * image_imag
-            step_real = pre[...] * resid_real
-            step_imag = pre[...] * resid_imag
-            send_small(
-                slot_a(step + 1, band),
-                [lane_sums(resid_real * step_real + resid_imag * step_imag) * inverse_total],
+            send_step(
+                4 + 2 * step,
+                band,
+                resid[band, 0] - size * image_real,
+                resid[band, 1] - size * image_imag,
             )
-            resid[band, 0] = resid_real
-            resid[band, 1] = resid_imag
-            send_real(4 + 2 * step, band, step_real, step_imag)
-            step_size[band] = size
+            added = size * overlap[band]
+            total[...] = added if step == 0 and band == 0 else total[...] + added
+            for c in range(2):
+                moved = size * search[band, c]
+                answer[band, c] = moved if step == 0 else answer[band, c] + moved
+
 
     columns = left_dot(basis_y[0], total[...])
     moved = [left_dot(basis_y[0], overlap[band]) for band in range(BANDS)]
     for band in range(BANDS):
-        step_size[band] = finish_curvature(CG_STEPS - 1, band)[0]
+        step_size[band] = finish_curvature(band, receive_small(1 + band, 5))
         columns = columns + step_size[band] * moved[band]
 
     slot = 2 * local
@@ -618,11 +628,21 @@
 
     for phase in range(2 * CG_STEPS + 1):
         for band in range(BANDS):
-            wait_bytes(send.at[phase, band, pl.ds(0, parts - 1)], bulk_out.at[phase, band])
-    for slot in range(1 + 2 * BANDS * CG_STEPS):
+            wait_bytes(recv.at[phase, band, pl.ds(0, bulk_rows(phase))], bulk_out.at[phase, band])
+    for slot in range(1 + BANDS):
         wait_bytes(small_recv.at[slot, pl.ds(0, parts - 1)], small_out.at[slot])
     for which in range(3):
         wait_bytes(go_recv.at[pl.ds(0, local * (devices - 1))], turn_out.at[which])
+
+
+def hand_over(coeff, density, hxc, coeff_out, density_out, hxc_out, done):
+    pairs = [(density, density_out), (hxc, hxc_out)]
+    pairs += [(coeff.at[b, c], coeff_out.at[b, c]) for b in range(BANDS) for c in range(2)]
+    copies = [pltpu.make_async_copy(a, b, done.at[i]) for i, (a, b) in enumerate(pairs)]
+    for copy in copies:
+        copy.start()
+    for copy in copies:
+        copy.wait()
 
 
 def body(wave_coeff, band_energy, local_potential, perturbation, xc_kernel, parts, pools):
@@ -631,7 +651,8 @@
     block = 2 * local * local
     wide = local * n
     phases = 2 * CG_STEPS + 1
-    slots = 1 + 2 * BANDS * CG_STEPS
+    room = block + 8
+    slots = 1 + BANDS
     slot_rows = 2 * local * parts
     grid = (4, 4, 2) if parts == 32 else (1, parts, 1)
     operands = [
@@ -663,10 +684,11 @@
             field,
             field,
             field,
+            field,
             pltpu.VMEM((BANDS, n, wide), f32),
             pltpu.VMEM((n, wide), f32),
-            pltpu.VMEM((phases, BANDS, parts, block, n), f32),
-            pltpu.VMEM((phases, BANDS, parts * block, n), f32),
+            pltpu.VMEM((phases, BANDS, parts, room, n), f32),
+            pltpu.VMEM((phases, BANDS, parts * room, n), f32),
             pltpu.VMEM((slots, 1, n), f32),
             pltpu.VMEM((slots, parts, 1, n), f32),
             pltpu.VMEM((pools * slot_rows, n), f32),
@@ -685,6 +707,14 @@
             collective_id=0, has_side_effects=True, vmem_limit_bytes=56 * 1024 * 1024
         ),
     )(operands[0], band_energy, *operands[1:])
+    results = [coeff, density, hxc]
+    coeff, density, hxc = pl.pallas_call(
+        hand_over,
+        out_shape=[jax.ShapeDtypeStruct(t.shape, f32) for t in results],
+        in_specs=[anywhere] * 3,
+        out_specs=[anywhere] * 3,
+        scratch_shapes=[dma((2 * BANDS + 2,))],
+    )(*results)
     return coeff.reshape(wave_coeff.shape), density, hxc
 
 

time: 138 us -> 178 us (1.29)
  Pallas kernels: 133 us -> 177 us
  local copies, waits for them, and re-layouts: 3.73 us -> 0 us
    pallas_call x0 -> x1, Pallas kernels: none -> 48.8 us  [body(): pl.pallas_call(hand_over, out_shape=[jax.ShapeDtypeStruct(t.shape, f32) f...]
    pallas_call x1, Pallas kernels: 133 us -> 128 us  [body(): pl.pallas_call(functools.partial(kernel, n, parts, pools, grid), out_shap...]
    unnamed x7 -> x0, local copies, waits for them, and re-layouts: 3.73 us -> none
where the time goes in v3:
time: 178 us
  Pallas kernels  177 us (99%)
    pallas_call x1, Pallas kernels, body(): pl.pallas_call(functools.partial(kernel, n, parts, pools, grid), out_shap...  128 us
    pallas_call x1, Pallas kernels, body(): pl.pallas_call(hand_over, out_shape=[jax.ShapeDtypeStruct(t.shape, f32) f...  48.8 us

profile of v3, /device:TPU:1, one launch (start us, length us, event | category | flops | bytes accessed | tf_op | source)
XLA Modules:
  0.0 177.7 jit_solution(4854795043976616174)
XLA Ops:
  0.6 128.1 %shard_map.130 = (f32[2,2,512,128]{3,2,1,0:T(8,128)}, f32[4,128,128]{2,1,0:T(8,128)}, f32[4,128,128]{2,1,0:T(8,128)}) custom-call(f32[2,2,512,128]{3,2,1,0:T(8,128)} %bitcast.2, f32[1,2]{1,0:T(1,128)} %energy.1, f32[4,128,128]{2,1,0:T(8,128)} %potential_hbm.1, f32[4,128,128]{2,1,0:T(8,128)} %perturbation_hbm.1, f32[4,128,128]{2,1,0:T(8,128)} %xc_hbm.1, ...), custom_call_target="tpu_custom_call" | custom-call | tf_op jit(solution)/shard_map/pallas_call | solution.py:668
  128.8 48.8 %shard_map.131 = (f32[2,2,512,128]{3,2,1,0:T(8,128)}, f32[4,128,128]{2,1,0:T(8,128)}, f32[4,128,128]{2,1,0:T(8,128)}) custom-call(f32[2,2,512,128]{3,2,1,0:T(8,128)} %get-tuple-element.9.coeff, f32[4,128,128]{2,1,0:T(8,128)} %get-tuple-element.10.density, f32[4,128,128]{2,1,0:T(8,128)} %get-tuple-element.11.hxc), custom_call_target="tpu_custom_call" | custom-call | tf_op jit(solution)/shard_map/pallas_call | solution.py:711

commit v4 on v3

--- a/solution.py
+++ b/solution.py
@@ -12,6 +12,7 @@
 
 CG_STEPS = 3
 BANDS = 2
+HALVES = 2
 cell_length = 51.3
 unit = 2.0 * math.pi / cell_length
 MESH = pl.DeviceIdType.MESH
@@ -50,14 +51,17 @@
     local = n // parts
     natural = [(c, j) for c in range(2) for j in range(n)]
     by_owner = [(c, q * local + m) for q in range(parts) for c in range(2) for m in range(local)]
-    by_local = [(c, q * local + m) for c in range(2) for m in range(local) for q in range(parts)]
-    scale = 1.0 / n**3
-    left = np.stack(
+    split = np.array_split(np.arange(local), HALVES)
+    by_local = [
+        [(c, q * local + m) for c in range(2) for m in ms for q in range(parts)] for ms in split
+    ]
+    outgoing = np.stack(
+        [split_table(left_table(by_owner, natural, n, sign), 1) for sign in (1.0, -1.0)]
+    )
+    incoming = np.stack(
         [
-            split_table(left_table(by_owner, natural, n, 1.0), 1),
-            split_table(left_table(natural, by_local, n, 1.0, scale), 1),
-            split_table(left_table(by_owner, natural, n, -1.0), 1),
-            split_table(left_table(natural, by_local, n, -1.0), 1),
+            np.stack([split_table(left_table(natural, cols, n, sign, size), 1) for cols in by_local])
+            for sign, size in ((1.0, 1.0 / n**3), (-1.0, 1.0))
         ]
     )
     right = np.stack(
@@ -84,7 +88,7 @@
     basis_z = np.stack([split_table(rows.T, 0), split_table(back, 0)])
     basis_x = split_table(x_rows, 1)
     spread_x = split_table(x_back.reshape(2 * n, n), 1)
-    return [left, right, basis_y, basis_x, spread_x, basis_z]
+    return [outgoing, right, incoming, basis_y, basis_x, spread_x, basis_z]
 
 
 def halves(value):
@@ -107,14 +111,14 @@
     n,
     parts,
     pools,
-    grid,
     raw_hbm,
     energy,
     potential_hbm,
     perturbation_hbm,
     xc_hbm,
-    left_hbm,
+    outgoing_hbm,
     right_hbm,
+    incoming_hbm,
     basis_y_hbm,
     basis_x_hbm,
     spread_x_hbm,
@@ -126,8 +130,9 @@
     potential,
     perturbation,
     xc,
-    left,
+    outgoing,
     right,
+    incoming,
     basis_y,
     basis_x,
     spread_x,
@@ -160,42 +165,38 @@
     turn_in,
 ):
     local = n // parts
-    block = 2 * local * local
+    group = local // HALVES
+    block = 2 * local * group
     room = block + 8
     devices = parts * pools
     inverse_total = 1.0 / n**3
     me = lax.axis_index("fft")
     pool = lax.axis_index("pool")
-    size_z, size_x, size_c = grid
-    my_z, my_x, my_c = me // (size_x * size_c), lax.rem(me // size_c, size_x), lax.rem(me, size_c)
-    at_self = (-(size_z // 2) % size_z) * size_x * size_c + (-(size_x // 2) % size_x) * size_c
-
     def lanes(value, index):
         return value[:, index * n : (index + 1) * n]
 
-    def peer(index):
-        z = lax.rem(my_z + size_z // 2 + index // (size_x * size_c), size_z)
-        x = lax.rem(my_x + size_x // 2 + lax.rem(index // size_c, size_x), size_x)
-        c = lax.rem(my_c + lax.rem(index, size_c), size_c)
-        return (z * size_x + x) * size_c + c
+    def turned(start, shift, size):
+        index = start + shift
+        return jnp.where(index >= size, index - size, index)
 
     def for_peers(act):
-        def step(index, _):
-            act(peer(index))
+        def step(shift, _):
+            act(turned(me, shift, parts))
             return 0
 
-        lax.fori_loop(0, at_self, step, 0)
-        lax.fori_loop(at_self + 1, parts, step, 0)
+        lax.fori_loop(parts // 2, parts, step, 0)
+        lax.fori_loop(1, parts // 2, step, 0)
 
     def for_devices(act):
-        for shift in (2, 1, 3):
-            other_pool = lax.rem(pool + shift, pools)
-
-            def step(index, _, other_pool=other_pool):
-                act(peer(index), other_pool)
+        for pool_shift in (2, 1, 3):
+            other_pool = turned(pool, pool_shift, pools)
+
+            def step(shift, _, other_pool=other_pool):
+                act(turned(me, shift, parts), other_pool)
                 return 0
 
-            lax.fori_loop(0, parts, step, 0)
+            lax.fori_loop(parts // 2, parts, step, 0)
+            lax.fori_loop(0, parts // 2, step, 0)
         for_peers(lambda other: act(other, pool))
 
     barrier = pltpu.get_barrier_semaphore()
@@ -210,7 +211,8 @@
     order = [
         (raw_hbm, raw),
         (right_hbm, right),
-        (left_hbm, left),
+        (outgoing_hbm, outgoing),
+        (incoming_hbm, incoming),
         (perturbation_hbm, perturbation),
         (potential_hbm, potential),
         (basis_y_hbm, basis_y),
@@ -224,52 +226,60 @@
         loads[i].start()
 
 
-    def store_bulk(phase, band, value):
-        for m in range(local):
-            send[phase, band, :, 2 * local * m : 2 * local * (m + 1), :] = lanes(value, m).reshape(
-                parts, 2 * local, n
-            )
-
-    def start_bulk(phase, band, row=None):
+    def row_half(phase):
+        return phase % 2 if phase >= 2 else None
+
+    def used_rows(phase, half):
+        return block + 1 if half == row_half(phase) else block
+
+    def store_half(phase, band, half, value, row=None):
+        for m in range(group):
+            send[phase, band, half, :, 2 * local * m : 2 * local * (m + 1), :] = lanes(
+                value, m
+            ).reshape(parts, 2 * local, n)
+        if half == row_half(phase):
+            send[phase, band, half, :, block:room, :] = jnp.broadcast_to(row, (parts, 8, n))
+
+    def start_half(phase, band, half):
         here = pl.multiple_of(me * room, room)
-        used = block if row is None else block + 1
-        if row is not None:
-            send[phase, band, :, block : block + 8, :] = jnp.broadcast_to(row, (parts, 8, n))
+        used = used_rows(phase, half)
 
         def start(other):
             pltpu.make_async_remote_copy(
-                src_ref=send.at[phase, band, other, pl.ds(0, used)],
-                dst_ref=recv.at[phase, band, pl.ds(here, used)],
-                send_sem=bulk_out.at[phase, band],
-                recv_sem=bulk_in.at[phase, band],
+                src_ref=send.at[phase, band, half, other, pl.ds(0, used)],
+                dst_ref=recv.at[phase, band, half, pl.ds(here, used)],
+                send_sem=bulk_out.at[phase, band, half],
+                recv_sem=bulk_in.at[phase, band, half],
                 device_id={"fft": other},
                 device_id_type=MESH,
             ).start()
 
         for_peers(start)
-        recv[phase, band, pl.ds(here, room), :] = send[phase, band, me]
-
-    def send_bulk(phase, band, value, row=None):
-        store_bulk(phase, band, value)
-        start_bulk(phase, band, row)
-
-    def bulk_rows(phase):
-        return (parts - 1) * (block + 1 if phase >= 2 else block)
+        recv[phase, band, half, pl.ds(here, room), :] = send[phase, band, half, me]
+
+    def half_bytes(phase, band, half):
+        return recv.at[phase, band, half, pl.ds(0, (parts - 1) * used_rows(phase, half))]
 
     def wait_bytes(ref, sem):
         pltpu.make_async_copy(ref, ref, sem).wait()
 
-    def receive_bulk(phase, band):
-        wait_bytes(recv.at[phase, band, pl.ds(0, bulk_rows(phase))], bulk_in.at[phase, band])
-        rows = []
-        for c in range(2):
-            for m in range(local):
-                pieces = []
-                for other in range(local):
-                    first = 2 * local * m + local * c + other
-                    pieces.append(recv[phase, band, pl.ds(first, parts, stride=room), :])
-                rows.append(jnp.concatenate(pieces, axis=1))
-        return jnp.concatenate(rows, axis=0)
+    def receive_bulk(phase, band, tables):
+        out = None
+        for half in range(HALVES):
+            wait_bytes(half_bytes(phase, band, half), bulk_in.at[phase, band, half])
+            rows = []
+            for c in range(2):
+                for m in range(group):
+                    pieces = []
+                    for other in range(local):
+                        first = 2 * local * m + local * c + other
+                        pieces.append(
+                            recv[phase, band, half, pl.ds(first, parts, stride=room), :]
+                        )
+                    rows.append(jnp.concatenate(pieces, axis=1))
+            part = left_dot(tables[half], jnp.concatenate(rows, axis=0))
+            out = part if out is None else out + part
+        return out
 
     row_id = lax.broadcasted_iota(jnp.int32, (8, n), 0)
     lane_id = lax.broadcasted_iota(jnp.int32, (8, n), 1)
@@ -295,7 +305,7 @@
         ]
 
     def bulk_row(phase, band, count):
-        rows = recv[phase, band, pl.ds(block, parts, stride=room), :]
+        rows = recv[phase, band, row_half(phase), pl.ds(block, parts, stride=room), :]
         return unpack(jnp.sum(rows, axis=0, keepdims=True), count)
 
     def send_small(slot, values):
@@ -321,30 +331,43 @@
 
 
     def along_z(real, imag, table):
+        count = real.shape[1] // n
         rows = jnp.concatenate(
-            [jnp.concatenate([lanes(real, m), lanes(imag, m)], axis=1) for m in range(local)],
+            [jnp.concatenate([lanes(real, m), lanes(imag, m)], axis=1) for m in range(count)],
             axis=0,
         )
         out = right_dot(rows, table)
-        picked = [out[m * n : (m + 1) * n] for m in range(local)]
+        picked = [out[m * n : (m + 1) * n] for m in range(count)]
         return (
             jnp.concatenate([lanes(v, 0) for v in picked], axis=1),
             jnp.concatenate([lanes(v, 1) for v in picked], axis=1),
         )
 
-    def send_real(phase, band, real, imag, row):
-        real, imag = along_z(real, imag, right[0])
-        send_bulk(phase, band, left_dot(left[0], jnp.concatenate([real, imag], axis=0)), row)
+    def half_of(value, half):
+        return value[:, half * group * n : (half + 1) * group * n]
+
+    def send_real(phase, band, real, imag, row=None):
+        for half in range(HALVES):
+            part = jnp.concatenate(
+                along_z(half_of(real, half), half_of(imag, half), right[0]), axis=0
+            )
+            store_half(phase, band, half, left_dot(outgoing[0], part), row)
+            if phase == 0 and band == 0 and half == 0:
+                pl.semaphore_wait(barrier, devices - 1)
+            start_half(phase, band, half)
 
     def receive_real(phase, band):
-        out = left_dot(left[1], receive_bulk(phase, band))
+        out = receive_bulk(phase, band, incoming[0])
         return out[:n], out[n:]
 
     def send_reciprocal(phase, band, real, imag, row=None):
-        send_bulk(phase, band, left_dot(left[2], jnp.concatenate([real, imag], axis=0)), row)
+        for half in range(HALVES):
+            part = jnp.concatenate([half_of(real, half), half_of(imag, half)], axis=0)
+            store_half(phase, band, half, left_dot(outgoing[1], part), row)
+            start_half(phase, band, half)
 
     def receive_reciprocal(phase, band):
-        out = left_dot(left[3], receive_bulk(phase, band))
+        out = receive_bulk(phase, band, incoming[1])
         return along_z(out[:n], out[n:], right[1])
 
 
@@ -358,11 +381,7 @@
         if band == 0:
             loads[1].wait()
             loads[2].wait()
-        real, imag = along_z(wave[band, 0], wave[band, 1], right[0])
-        store_bulk(0, band, left_dot(left[0], jnp.concatenate([real, imag], axis=0)))
-        if band == 0:
-            pl.semaphore_wait(barrier, devices - 1)
-        start_bulk(0, band)
+        send_real(0, band, wave[band, 0], wave[band, 1])
 
     def wavenumber(index):
         signed = jnp.where(2 * index >= n, index - n, index)
@@ -628,33 +647,40 @@
 
     for phase in range(2 * CG_STEPS + 1):
         for band in range(BANDS):
-            wait_bytes(recv.at[phase, band, pl.ds(0, bulk_rows(phase))], bulk_out.at[phase, band])
+            for half in range(HALVES):
+                wait_bytes(half_bytes(phase, band, half), bulk_out.at[phase, band, half])
     for slot in range(1 + BANDS):
         wait_bytes(small_recv.at[slot, pl.ds(0, parts - 1)], small_out.at[slot])
     for which in range(3):
         wait_bytes(go_recv.at[pl.ds(0, local * (devices - 1))], turn_out.at[which])
 
 
-def hand_over(coeff, density, hxc, coeff_out, density_out, hxc_out, done):
-    pairs = [(density, density_out), (hxc, hxc_out)]
-    pairs += [(coeff.at[b, c], coeff_out.at[b, c]) for b in range(BANDS) for c in range(2)]
-    copies = [pltpu.make_async_copy(a, b, done.at[i]) for i, (a, b) in enumerate(pairs)]
-    for copy in copies:
+def hand_over(coeff, density, hxc, coeff_out, density_out, hxc_out, *scratch):
+    held, held_density, held_hxc, came, gone = scratch
+    moves = [(density, held_density, density_out), (hxc, held_hxc, hxc_out)]
+    for b in range(BANDS):
+        for c in range(2):
+            moves.append((coeff.at[b, c], held.at[b, c], coeff_out.at[b, c]))
+    first = [pltpu.make_async_copy(a, h, came.at[i]) for i, (a, h, _) in enumerate(moves)]
+    second = [pltpu.make_async_copy(h, o, gone.at[i]) for i, (_, h, o) in enumerate(moves)]
+    for copy in first:
         copy.start()
-    for copy in copies:
+    for copy, onward in zip(first, second):
+        copy.wait()
+        onward.start()
+    for copy in second:
         copy.wait()
 
 
 def body(wave_coeff, band_energy, local_potential, perturbation, xc_kernel, parts, pools):
     n = wave_coeff.shape[-1]
     local = n // parts
-    block = 2 * local * local
+    block = 2 * local * (local // HALVES)
     wide = local * n
     phases = 2 * CG_STEPS + 1
     room = block + 8
     slots = 1 + BANDS
     slot_rows = 2 * local * parts
-    grid = (4, 4, 2) if parts == 32 else (1, parts, 1)
     operands = [
         wave_coeff.reshape(BANDS, 2, n * local, n),
         local_potential,
@@ -666,13 +692,13 @@
     field = pltpu.VMEM((BANDS, 2, n, wide), f32)
     dma = pltpu.SemaphoreType.DMA
     coeff, density, hxc = pl.pallas_call(
-        functools.partial(kernel, n, parts, pools, grid),
+        functools.partial(kernel, n, parts, pools),
         out_shape=(
             jax.ShapeDtypeStruct(operands[0].shape, f32),
             jax.ShapeDtypeStruct((local, n, n), f32),
             jax.ShapeDtypeStruct((local, n, n), f32),
         ),
-        in_specs=[anywhere, pl.BlockSpec(memory_space=pltpu.SMEM)] + [anywhere] * 9,
+        in_specs=[anywhere, pl.BlockSpec(memory_space=pltpu.SMEM)] + [anywhere] * 10,
         out_specs=(vmem, vmem, vmem),
         scratch_shapes=[pltpu.VMEM(t.shape, t.dtype) for t in operands]
         + [
@@ -687,17 +713,17 @@
             field,
             pltpu.VMEM((BANDS, n, wide), f32),
             pltpu.VMEM((n, wide), f32),
-            pltpu.VMEM((phases, BANDS, parts, room, n), f32),
-            pltpu.VMEM((phases, BANDS, parts * room, n), f32),
+            pltpu.VMEM((phases, BANDS, HALVES, parts, room, n), f32),
+            pltpu.VMEM((phases, BANDS, HALVES, parts * room, n), f32),
             pltpu.VMEM((slots, 1, n), f32),
             pltpu.VMEM((slots, parts, 1, n), f32),
             pltpu.VMEM((pools * slot_rows, n), f32),
             pltpu.VMEM((pools * slot_rows, n), f32),
             pltpu.VMEM((2, slot_rows, n), f32),
             pltpu.VMEM((2, pools * slot_rows, n), f32),
-            dma((10,)),
-            dma((phases, BANDS)),
-            dma((phases, BANDS)),
+            dma((11,)),
+            dma((phases, BANDS, HALVES)),
+            dma((phases, BANDS, HALVES)),
             dma((slots,)),
             dma((slots,)),
             dma((3,)),
@@ -713,7 +739,8 @@
         out_shape=[jax.ShapeDtypeStruct(t.shape, f32) for t in results],
         in_specs=[anywhere] * 3,
         out_specs=[anywhere] * 3,
-        scratch_shapes=[dma((2 * BANDS + 2,))],
+        scratch_shapes=[pltpu.VMEM(t.shape, f32) for t in results]
+        + [dma((2 * BANDS + 2,)), dma((2 * BANDS + 2,))],
     )(*results)
     return coeff.reshape(wave_coeff.shape), density, hxc
 

time: 178 us -> 124 us (0.70)
  Pallas kernels: 177 us -> 123 us
    pallas_call x1, Pallas kernels: 48.8 us -> 2.19 us  [body(): pl.pallas_call(hand_over, out_shape=[jax.ShapeDtypeStruct(t.shape, f32) f...]
    pallas_call x1, Pallas kernels: 128 us -> 121 us  [body(): pl.pallas_call(functools.partial(kernel, n, parts, pools), out_shape=(jax...]
where the time goes in v4:
time: 124 us
  Pallas kernels  123 us (99%)
    pallas_call x1, Pallas kernels, body(): pl.pallas_call(functools.partial(kernel, n, parts, pools), out_shape=(jax...  121 us

profile of v4, /device:TPU:1, one launch (start us, length us, event | category | flops | bytes accessed | tf_op | source)
XLA Modules:
  0.0 123.6 jit_solution(13896800543400580214)
XLA Ops:
  0.6 120.6 %shard_map.139 = (f32[2,2,512,128]{3,2,1,0:T(8,128)}, f32[4,128,128]{2,1,0:T(8,128)}, f32[4,128,128]{2,1,0:T(8,128)}) custom-call(f32[2,2,512,128]{3,2,1,0:T(8,128)} %bitcast.2, f32[1,2]{1,0:T(1,128)} %energy.1, f32[4,128,128]{2,1,0:T(8,128)} %potential_hbm.1, f32[4,128,128]{2,1,0:T(8,128)} %perturbation_hbm.1, f32[4,128,128]{2,1,0:T(8,128)} %xc_hbm.1, ...), custom_call_target="tpu_custom_call" | custom-call | tf_op jit(solution)/shard_map/pallas_call | solution.py:694
  121.3 2.2 %shard_map.140 = (f32[2,2,512,128]{3,2,1,0:T(8,128)}, f32[4,128,128]{2,1,0:T(8,128)}, f32[4,128,128]{2,1,0:T(8,128)}) custom-call(f32[2,2,512,128]{3,2,1,0:T(8,128)} %get-tuple-element.9.coeff, f32[4,128,128]{2,1,0:T(8,128)} %get-tuple-element.10.density, f32[4,128,128]{2,1,0:T(8,128)} %get-tuple-element.11.hxc), custom_call_target="tpu_custom_call" | custom-call | tf_op jit(solution)/shard_map/pallas_call | solution.py:737

commit v5 on v4

--- a/solution.py
+++ b/solution.py
@@ -163,6 +163,7 @@
     small_in,
     turn_out,
     turn_in,
+    met,
 ):
     local = n // parts
     group = local // HALVES
@@ -206,7 +207,9 @@
             barrier, inc=1, device_id={"pool": other_pool, "fft": other}, device_id_type=MESH
         )
 
-    for_devices(greet)
+    for_peers(lambda other: greet(other, pool))
+    for pool_shift in range(1, pools):
+        greet(me, turned(pool, pool_shift, pools))
     loads = {}
     order = [
         (raw_hbm, raw),
@@ -353,7 +356,7 @@
             )
             store_half(phase, band, half, left_dot(outgoing[0], part), row)
             if phase == 0 and band == 0 and half == 0:
-                pl.semaphore_wait(barrier, devices - 1)
+                pl.semaphore_wait(barrier, parts + pools - 2)
             start_half(phase, band, half)
 
     def receive_real(phase, band):
@@ -382,6 +385,14 @@
             loads[1].wait()
             loads[2].wait()
         send_real(0, band, wave[band, 0], wave[band, 1])
+
+    for pool_shift in range(1, pools):
+        pl.semaphore_signal(
+            met,
+            inc=1,
+            device_id={"pool": turned(pool, pool_shift, pools), "fft": me},
+            device_id_type=MESH,
+        )
 
     def wavenumber(index):
         signed = jnp.where(2 * index >= n, index - n, index)
@@ -475,12 +486,12 @@
 
     step_size = [None] * BANDS
 
-    def finish_curvature(band, values):
+    def finish_curvature(product, values):
         curvature, c0_real, c0_imag, c1_real, c1_imag = values
         curvature = curvature + 2.0 * (
             c0_real * c0_real + c0_imag * c0_imag + c1_real * c1_real + c1_imag * c1_imag
         )
-        return rho[band] / curvature
+        return product / curvature
 
     for step in range(CG_STEPS):
         last = step + 1 == CG_STEPS
@@ -508,9 +519,9 @@
             image_real = level * real
             image_imag = level * imag
             sums[0] = sums[0] + lane_sums(image_real * real + image_imag * imag)
-            if last:
+            if last and band + 1 < BANDS:
                 send_small(1 + band, sums)
-            else:
+            if not last:
                 send_reciprocal(3 + 2 * step, band, image_real, image_imag, pack(sums))
             overlap[band] = space_wave[band, 0] * real + space_wave[band, 1] * imag
             for c in range(2):
@@ -518,13 +529,16 @@
                     search[band, c] = ahead[band, c]
                 else:
                     search[band, c] = ahead[band, c] + beta * search[band, c]
+            if last and band == 0:
+                base = left_dot(basis_y[0], total[...])
+                moved = left_dot(basis_y[0], overlap[band])
         if last:
             break
         for band in range(BANDS):
             pot_real, pot_imag = receive_reciprocal(3 + 2 * step, band)
             values = bulk_row(3 + 2 * step, band, 5)
             _, c0_real, c0_imag, c1_real, c1_imag = values
-            size = finish_curvature(band, values)
+            size = finish_curvature(rho[band], values)
             shifted = kin[...] - energy[0, band]
             real = search[band, 0]
             imag = search[band, 1]
@@ -563,25 +577,19 @@
                 answer[band, c] = moved if step == 0 else answer[band, c] + moved
 
 
-    columns = left_dot(basis_y[0], total[...])
-    moved = [left_dot(basis_y[0], overlap[band]) for band in range(BANDS)]
-    for band in range(BANDS):
-        step_size[band] = finish_curvature(band, receive_small(1 + band, 5))
-        columns = columns + step_size[band] * moved[band]
-
     slot = 2 * local
 
-    def turn(which, source, target, all_columns):
+    def turn(which, source, target, all_columns, rows=local):
         here = pl.multiple_of((pool * parts + me) * slot, slot)
         own = here if all_columns else pl.multiple_of(me * slot, slot)
-        target[pl.ds(here, local), :] = source[pl.ds(own, local), :]
+        target[pl.ds(here, rows), :] = source[pl.ds(own, rows), :]
 
         def start(other, other_pool):
             there = other_pool * parts + other if all_columns else other
             there = pl.multiple_of(there * slot, slot)
             pltpu.make_async_remote_copy(
-                src_ref=source.at[pl.ds(there, local)],
-                dst_ref=target.at[pl.ds(here, local)],
+                src_ref=source.at[pl.ds(there, rows)],
+                dst_ref=target.at[pl.ds(here, rows)],
                 send_sem=turn_out.at[which],
                 recv_sem=turn_in.at[which],
                 device_id={"pool": other_pool, "fft": other},
@@ -590,52 +598,74 @@
 
         for_devices(start)
 
-    def wait_turn(which, target):
-        wait_bytes(target.at[pl.ds(0, local * (devices - 1))], turn_in.at[which])
-
+    def wait_turn(which, target, rows=local):
+        wait_bytes(target.at[pl.ds(0, rows * (devices - 1))], turn_in.at[which])
+
+    pl.semaphore_wait(met, pools - 1)
+    step_size[0] = finish_curvature(rho[0], receive_small(1, 5))
+    columns = base + step_size[0] * moved
     for m in range(local):
-        go_send[pl.ds(m, devices, stride=slot), :] = lanes(columns, m)
-    turn(0, go_send, go_recv, True)
+        go_send[0, pl.ds(m, devices, stride=slot), :] = lanes(columns, m)
+    turn(0, go_send.at[0], go_recv.at[0], True)
+    columns = left_dot(basis_y[0], overlap[1])
+    for m in range(local):
+        go_send[1, pl.ds(m, devices, stride=slot), :] = lanes(columns, m)
+    share = jnp.where(lane_id[:1] == 0, rho[1] * (1.0 / parts), 0.0)
+    go_send[1, pl.ds(local, devices, stride=slot), :] = jnp.broadcast_to(
+        pack(sums + [share]), (devices, n)
+    )
+    turn(1, go_send.at[1], go_recv.at[1], True, local + 1)
+
+    even = 2 * me
+    frequency = jnp.where(
+        pool == 0, even, jnp.where(pool == 1, jnp.where(me == 0, n // 2, even), even + 1)
+    )
+
+    def plain_square(index):
+        k = jnp.where(index > n // 2, index - n // 2, index)
+        return (k.astype(f32) * unit) ** 2
+
+    squared = (
+        plain_square(index_x) + (frequency.astype(f32) * unit) ** 2 + plain_square(index_z)
+    )
+    nonzero = (squared > 0).astype(f32)
+    coulomb = 4.0 * math.pi * nonzero / (squared + (1.0 - nonzero))
+
+    wait_turn(0, go_recv.at[0])
+    wait_turn(1, go_recv.at[1], local + 1)
+    sizes = []
+    for other in range(pools):
+        first = other * parts * slot + local
+        rows = go_recv[1, pl.ds(first, parts, stride=slot), :]
+        values = unpack(jnp.sum(rows, axis=0, keepdims=True), 6)
+        sizes.append(finish_curvature(values[5], values[:5]))
+    pieces = []
+    for m in range(local):
+        piece = None
+        for other in range(pools):
+            rows = pl.ds(other * parts * slot + m, parts, stride=slot)
+            term = go_recv[0, rows, :] + sizes[other] * go_recv[1, rows, :]
+            piece = term if piece is None else piece + term
+        back_send[0, pl.ds(m, parts, stride=slot), :] = piece
+        pieces.append(piece)
+    turn(2, back_send.at[0], back_recv.at[0], False)
+
+
+    field = left_dot(basis_x[...], jnp.concatenate(pieces, axis=0))
+    field = coulomb * right_dot(field, basis_z[0])
+    field = left_dot(spread_x[...], right_dot(field, basis_z[1]))
+    back_send[1] = field
+    turn(3, back_send.at[1], back_recv.at[1], False)
+
+    step_size[1] = sum(jnp.where(pool == i, sizes[i], 0.0) for i in range(pools))
     for band in range(BANDS):
         for c in range(2):
             value = answer[band, c] + step_size[band] * search[band, c]
             for m in range(local):
                 coeff[band, c, pl.ds(m, n, stride=local), :] = lanes(value, m)
 
-    even = 2 * me
-    frequency = jnp.where(
-        pool == 0, even, jnp.where(pool == 1, jnp.where(me == 0, n // 2, even), even + 1)
-    )
-
-    def plain_square(index):
-        k = jnp.where(index > n // 2, index - n // 2, index)
-        return (k.astype(f32) * unit) ** 2
-
-    squared = (
-        plain_square(index_x) + (frequency.astype(f32) * unit) ** 2 + plain_square(index_z)
-    )
-    nonzero = (squared > 0).astype(f32)
-    coulomb = 4.0 * math.pi * nonzero / (squared + (1.0 - nonzero))
-
-    wait_turn(0, go_recv)
-    pieces = []
-    for m in range(local):
-        piece = go_recv[pl.ds(m, parts, stride=slot), :]
-        for other in range(1, pools):
-            piece = piece + go_recv[pl.ds(other * parts * slot + m, parts, stride=slot), :]
-        back_send[0, pl.ds(m, parts, stride=slot), :] = piece
-        pieces.append(piece)
-    turn(1, back_send.at[0], back_recv.at[0], False)
-
-
-    field = left_dot(basis_x[...], jnp.concatenate(pieces, axis=0))
-    field = coulomb * right_dot(field, basis_z[0])
-    field = left_dot(spread_x[...], right_dot(field, basis_z[1]))
-    back_send[1] = field
-    turn(2, back_send.at[1], back_recv.at[1], False)
-
     for i, result in enumerate((density, hxc)):
-        wait_turn(1 + i, back_recv.at[i])
+        wait_turn(2 + i, back_recv.at[i])
         columns = [back_recv[i, pl.ds(m, devices, stride=slot), :] for m in range(local)]
         whole = left_dot(basis_y[1], jnp.concatenate(columns, axis=1))
         for m in range(local):
@@ -649,26 +679,20 @@
         for band in range(BANDS):
             for half in range(HALVES):
                 wait_bytes(half_bytes(phase, band, half), bulk_out.at[phase, band, half])
-    for slot in range(1 + BANDS):
+    for slot in range(BANDS):
         wait_bytes(small_recv.at[slot, pl.ds(0, parts - 1)], small_out.at[slot])
-    for which in range(3):
-        wait_bytes(go_recv.at[pl.ds(0, local * (devices - 1))], turn_out.at[which])
-
-
-def hand_over(coeff, density, hxc, coeff_out, density_out, hxc_out, *scratch):
-    held, held_density, held_hxc, came, gone = scratch
-    moves = [(density, held_density, density_out), (hxc, held_hxc, hxc_out)]
-    for b in range(BANDS):
-        for c in range(2):
-            moves.append((coeff.at[b, c], held.at[b, c], coeff_out.at[b, c]))
-    first = [pltpu.make_async_copy(a, h, came.at[i]) for i, (a, h, _) in enumerate(moves)]
-    second = [pltpu.make_async_copy(h, o, gone.at[i]) for i, (_, h, o) in enumerate(moves)]
-    for copy in first:
+    for which in range(4):
+        rows = local + 1 if which == 1 else local
+        wait_bytes(go_recv.at[0, pl.ds(0, rows * (devices - 1))], turn_out.at[which])
+
+
+def hand_over(coeff, density, hxc, coeff_out, density_out, hxc_out, gone):
+    moves = [(density, density_out), (hxc, hxc_out)]
+    moves += [(coeff.at[b, c], coeff_out.at[b, c]) for b in range(BANDS) for c in range(2)]
+    copies = [pltpu.make_async_copy(a, b, gone.at[i]) for i, (a, b) in enumerate(moves)]
+    for copy in copies:
         copy.start()
-    for copy, onward in zip(first, second):
-        copy.wait()
-        onward.start()
-    for copy in second:
+    for copy in copies:
         copy.wait()
 
 
@@ -679,7 +703,7 @@
     wide = local * n
     phases = 2 * CG_STEPS + 1
     room = block + 8
-    slots = 1 + BANDS
+    slots = BANDS
     slot_rows = 2 * local * parts
     operands = [
         wave_coeff.reshape(BANDS, 2, n * local, n),
@@ -694,9 +718,9 @@
     coeff, density, hxc = pl.pallas_call(
         functools.partial(kernel, n, parts, pools),
         out_shape=(
-            jax.ShapeDtypeStruct(operands[0].shape, f32),
-            jax.ShapeDtypeStruct((local, n, n), f32),
-            jax.ShapeDtypeStruct((local, n, n), f32),
+            pltpu.VMEM(operands[0].shape, f32),
+            pltpu.VMEM((local, n, n), f32),
+            pltpu.VMEM((local, n, n), f32),
         ),
         in_specs=[anywhere, pl.BlockSpec(memory_space=pltpu.SMEM)] + [anywhere] * 10,
         out_specs=(vmem, vmem, vmem),
@@ -717,8 +741,8 @@
             pltpu.VMEM((phases, BANDS, HALVES, parts * room, n), f32),
             pltpu.VMEM((slots, 1, n), f32),
             pltpu.VMEM((slots, parts, 1, n), f32),
-            pltpu.VMEM((pools * slot_rows, n), f32),
-            pltpu.VMEM((pools * slot_rows, n), f32),
+            pltpu.VMEM((2, pools * slot_rows, n), f32),
+            pltpu.VMEM((2, pools * slot_rows, n), f32),
             pltpu.VMEM((2, slot_rows, n), f32),
             pltpu.VMEM((2, pools * slot_rows, n), f32),
             dma((11,)),
@@ -726,8 +750,9 @@
             dma((phases, BANDS, HALVES)),
             dma((slots,)),
             dma((slots,)),
-            dma((3,)),
-            dma((3,)),
+            dma((4,)),
+            dma((4,)),
+            pltpu.SemaphoreType.REGULAR,
         ],
         compiler_params=pltpu.CompilerParams(
             collective_id=0, has_side_effects=True, vmem_limit_bytes=56 * 1024 * 1024
@@ -737,10 +762,9 @@
     coeff, density, hxc = pl.pallas_call(
         hand_over,
         out_shape=[jax.ShapeDtypeStruct(t.shape, f32) for t in results],
-        in_specs=[anywhere] * 3,
+        in_specs=[vmem] * 3,
         out_specs=[anywhere] * 3,
-        scratch_shapes=[pltpu.VMEM(t.shape, f32) for t in results]
-        + [dma((2 * BANDS + 2,)), dma((2 * BANDS + 2,))],
+        scratch_shapes=[dma((2 * BANDS + 2,))],
     )(*results)
     return coeff.reshape(wave_coeff.shape), density, hxc
 

time: 124 us -> 122 us (0.984)
  Pallas kernels: 123 us -> 119 us
  local copies, waits for them, and re-layouts: 0 us -> 2.37 us
    pallas_call x1, Pallas kernels: 121 us -> 117 us  [body(): pl.pallas_call(functools.partial(kernel, n, parts, pools), out_shape=(plt...]
    unnamed x0 -> x6, local copies, waits for them, and re-layouts: none -> 2.37 us
where the time goes in v5:
time: 122 us
  Pallas kernels  119 us (98%)
  local copies, waits for them, and re-layouts  2.37 us (2%)
    pallas_call x1, Pallas kernels, body(): pl.pallas_call(functools.partial(kernel, n, parts, pools), out_shape=(plt...  117 us
    pallas_call x1, Pallas kernels, body(): pl.pallas_call(hand_over, out_shape=[jax.ShapeDtypeStruct(t.shape, f32) f...  2.53 us

profile of v5, /device:TPU:1, one launch (start us, length us, event | category | flops | bytes accessed | tf_op | source)
XLA Modules:
  0.0 122.3 jit_solution(2836398594079103900)
XLA Ops:
  0.6 116.6 %shard_map.139 = (f32[2,2,512,128]{3,2,1,0:T(8,128)S(1)}, f32[4,128,128]{2,1,0:T(8,128)S(1)}, f32[4,128,128]{2,1,0:T(8,128)S(1)}) custom-call(f32[2,2,512,128]{3,2,1,0:T(8,128)} %bitcast.2, f32[1,2]{1,0:T(1,128)} %energy.1, f32[4,128,128]{2,1,0:T(8,128)} %potential_hbm.1, f32[4,128,128]{2,1,0:T(8,128)} %perturbation_hbm.1, f32[4,128,128]{2,1,0:T(8,128)} %xc_hbm.1, ...), custom_call_target="tpu_custom_call" | custom-call | tf_op jit(solution)/shard_map/pallas_call | solution.py:718
  117.2 0.0 copy-start
  117.2 1.0 copy-done
  118.2 0.0 copy-start.1
  118.2 0.7 copy-done.1
  118.9 0.0 copy-start.2
  118.9 0.7 copy-done.2
  119.6 2.5 %shard_map.140 = (f32[2,2,512,128]{3,2,1,0:T(8,128)}, f32[4,128,128]{2,1,0:T(8,128)}, f32[4,128,128]{2,1,0:T(8,128)}) custom-call(f32[2,2,512,128]{3,2,1,0:T(8,128)} %copy-done, f32[4,128,128]{2,1,0:T(8,128)} %copy-done.1, f32[4,128,128]{2,1,0:T(8,128)} %copy-done.2), custom_call_target="tpu_custom_call" | custom-call | tf_op jit(solution)/shard_map/pallas_call | solution.py:762
Async XLA Ops:
  117.2 1.0 copy-start
  118.2 0.7 copy-start.1
  118.9 0.7 copy-start.2

commit v6 on v4

--- a/solution.py
+++ b/solution.py
@@ -123,6 +123,9 @@
     basis_x_hbm,
     spread_x_hbm,
     basis_z_hbm,
+    coeff_out,
+    density_out,
+    hxc_out,
     coeff,
     density,
     hxc,
@@ -163,6 +166,8 @@
     small_in,
     turn_out,
     turn_in,
+    met,
+    stored,
 ):
     local = n // parts
     group = local // HALVES
@@ -206,7 +211,9 @@
             barrier, inc=1, device_id={"pool": other_pool, "fft": other}, device_id_type=MESH
         )
 
-    for_devices(greet)
+    for_peers(lambda other: greet(other, pool))
+    for pool_shift in range(1, pools):
+        greet(me, turned(pool, pool_shift, pools))
     loads = {}
     order = [
         (raw_hbm, raw),
@@ -227,7 +234,7 @@
 
 
     def row_half(phase):
-        return phase % 2 if phase >= 2 else None
+        return HALVES - 1 if phase >= 2 else None
 
     def used_rows(phase, half):
         return block + 1 if half == row_half(phase) else block
@@ -238,7 +245,9 @@
                 value, m
             ).reshape(parts, 2 * local, n)
         if half == row_half(phase):
-            send[phase, band, half, :, block:room, :] = jnp.broadcast_to(row, (parts, 8, n))
+            send[phase, band, half, :, block:room, :] = jnp.broadcast_to(
+                pack(row), (parts, 8, n)
+            )
 
     def start_half(phase, band, half):
         here = pl.multiple_of(me * room, room)
@@ -308,26 +317,26 @@
         rows = recv[phase, band, row_half(phase), pl.ds(block, parts, stride=room), :]
         return unpack(jnp.sum(rows, axis=0, keepdims=True), count)
 
-    def send_small(slot, values):
+    def send_small(values):
         row = pack(values)
-        small_send[slot] = row
-        small_recv[slot, me] = row
+        small_send[...] = row
+        small_recv[me] = row
 
         def start(other):
             pltpu.make_async_remote_copy(
-                src_ref=small_send.at[slot],
-                dst_ref=small_recv.at[slot, me],
-                send_sem=small_out.at[slot],
-                recv_sem=small_in.at[slot],
+                src_ref=small_send,
+                dst_ref=small_recv.at[me],
+                send_sem=small_out,
+                recv_sem=small_in,
                 device_id={"fft": other},
                 device_id_type=MESH,
             ).start()
 
         for_peers(start)
 
-    def receive_small(slot, count):
-        wait_bytes(small_recv.at[slot, pl.ds(0, parts - 1)], small_in.at[slot])
-        return unpack(jnp.sum(small_recv[slot], axis=0), count)
+    def receive_small(count):
+        wait_bytes(small_recv.at[pl.ds(0, parts - 1)], small_in)
+        return unpack(jnp.sum(small_recv[...], axis=0), count)
 
 
     def along_z(real, imag, table):
@@ -353,7 +362,7 @@
             )
             store_half(phase, band, half, left_dot(outgoing[0], part), row)
             if phase == 0 and band == 0 and half == 0:
-                pl.semaphore_wait(barrier, devices - 1)
+                pl.semaphore_wait(barrier, parts + pools - 2)
             start_half(phase, band, half)
 
     def receive_real(phase, band):
@@ -382,6 +391,14 @@
             loads[1].wait()
             loads[2].wait()
         send_real(0, band, wave[band, 0], wave[band, 1])
+
+    for pool_shift in range(1, pools):
+        pl.semaphore_signal(
+            met,
+            inc=1,
+            device_id={"pool": turned(pool, pool_shift, pools), "fft": me},
+            device_id_type=MESH,
+        )
 
     def wavenumber(index):
         signed = jnp.where(2 * index >= n, index - n, index)
@@ -421,7 +438,7 @@
             first_imag = space_wave[0, 1]
             overlaps.append(lane_sums(first_real * changed_real + first_imag * changed_imag))
             overlaps.append(lane_sums(first_real * changed_imag - first_imag * changed_real))
-            send_small(0, overlaps)
+            send_small(overlaps)
         send_reciprocal(1, band, changed_real, changed_imag)
 
     def products(band, real, imag):
@@ -438,7 +455,7 @@
     def send_step(phase, band, resid_real, resid_imag):
         real = pre[...] * resid_real
         imag = pre[...] * resid_imag
-        row = pack([lane_sums(resid_real * real + resid_imag * imag) * inverse_total])
+        row = [lane_sums(resid_real * real + resid_imag * imag) * inverse_total]
         resid[band, 0] = resid_real
         resid[band, 1] = resid_imag
         ahead[band, 0] = real
@@ -451,7 +468,7 @@
     for band in range(BANDS):
         real, imag = receive_reciprocal(1, band)
         if band == 0:
-            same0, same1, cross_real, cross_imag = receive_small(0, 4)
+            same0, same1, cross_real, cross_imag = receive_small(4)
         if band == 0:
             m0_real, m0_imag, m1_real, m1_imag = same0, 0.0 * same0, cross_real, -cross_imag
         else:
@@ -473,17 +490,58 @@
         send_step(2, band, resid_real, resid_imag)
 
 
-    step_size = [None] * BANDS
-
-    def finish_curvature(band, values):
+    def finish_curvature(product, values):
         curvature, c0_real, c0_imag, c1_real, c1_imag = values
         curvature = curvature + 2.0 * (
             c0_real * c0_real + c0_imag * c0_imag + c1_real * c1_real + c1_imag * c1_imag
         )
-        return rho[band] / curvature
+        return product / curvature
+
+
+    slot = 2 * local
+
+    def turn(which, source, target, all_columns, rows=local):
+        here = pl.multiple_of((pool * parts + me) * slot, slot)
+        own = here if all_columns else pl.multiple_of(me * slot, slot)
+        target[pl.ds(here, rows), :] = source[pl.ds(own, rows), :]
+
+        def start(other, other_pool):
+            there = other_pool * parts + other if all_columns else other
+            there = pl.multiple_of(there * slot, slot)
+            pltpu.make_async_remote_copy(
+                src_ref=source.at[pl.ds(there, rows)],
+                dst_ref=target.at[pl.ds(here, rows)],
+                send_sem=turn_out.at[which],
+                recv_sem=turn_in.at[which],
+                device_id={"pool": other_pool, "fft": other},
+                device_id_type=MESH,
+            ).start()
+
+        for_devices(start)
+
+    def wait_turn(which, target, rows=local):
+        wait_bytes(target.at[pl.ds(0, rows * (devices - 1))], turn_in.at[which])
+
+    def send_columns(which, value):
+        columns = left_dot(basis_y[0], value)
+        for m in range(local):
+            go_send[which, pl.ds(m, devices, stride=slot), :] = lanes(columns, m)
+
+    def send_term(band, sums):
+        which = 1 + band
+        send_columns(which, overlap[band])
+        share = jnp.where(lane_id[:1] == 0, rho[band] * (1.0 / parts), 0.0)
+        go_send[which, pl.ds(local, devices, stride=slot), :] = jnp.broadcast_to(
+            pack(sums + [share]), (devices, n)
+        )
+        turn(which, go_send.at[which], go_recv.at[which], True, local + 1)
 
     for step in range(CG_STEPS):
         last = step + 1 == CG_STEPS
+        if last:
+            pl.semaphore_wait(met, pools - 1)
+            send_columns(0, total[...])
+            turn(0, go_send.at[0], go_recv.at[0], True)
         for band in range(BANDS):
             real, imag = ahead[band, 0], ahead[band, 1]
             sums = [kinetic_sum(band, real, imag, real, imag)] + products(band, real, imag)
@@ -508,23 +566,23 @@
             image_real = level * real
             image_imag = level * imag
             sums[0] = sums[0] + lane_sums(image_real * real + image_imag * imag)
-            if last:
-                send_small(1 + band, sums)
-            else:
-                send_reciprocal(3 + 2 * step, band, image_real, image_imag, pack(sums))
+            if not last:
+                send_reciprocal(3 + 2 * step, band, image_real, image_imag, sums)
             overlap[band] = space_wave[band, 0] * real + space_wave[band, 1] * imag
             for c in range(2):
                 if step == 0:
                     search[band, c] = ahead[band, c]
                 else:
                     search[band, c] = ahead[band, c] + beta * search[band, c]
+            if last:
+                send_term(band, sums)
         if last:
             break
         for band in range(BANDS):
             pot_real, pot_imag = receive_reciprocal(3 + 2 * step, band)
             values = bulk_row(3 + 2 * step, band, 5)
             _, c0_real, c0_imag, c1_real, c1_imag = values
-            size = finish_curvature(band, values)
+            size = finish_curvature(rho[band], values)
             shifted = kin[...] - energy[0, band]
             real = search[band, 0]
             imag = search[band, 1]
@@ -562,46 +620,6 @@
                 moved = size * search[band, c]
                 answer[band, c] = moved if step == 0 else answer[band, c] + moved
 
-
-    columns = left_dot(basis_y[0], total[...])
-    moved = [left_dot(basis_y[0], overlap[band]) for band in range(BANDS)]
-    for band in range(BANDS):
-        step_size[band] = finish_curvature(band, receive_small(1 + band, 5))
-        columns = columns + step_size[band] * moved[band]
-
-    slot = 2 * local
-
-    def turn(which, source, target, all_columns):
-        here = pl.multiple_of((pool * parts + me) * slot, slot)
-        own = here if all_columns else pl.multiple_of(me * slot, slot)
-        target[pl.ds(here, local), :] = source[pl.ds(own, local), :]
-
-        def start(other, other_pool):
-            there = other_pool * parts + other if all_columns else other
-            there = pl.multiple_of(there * slot, slot)
-            pltpu.make_async_remote_copy(
-                src_ref=source.at[pl.ds(there, local)],
-                dst_ref=target.at[pl.ds(here, local)],
-                send_sem=turn_out.at[which],
-                recv_sem=turn_in.at[which],
-                device_id={"pool": other_pool, "fft": other},
-                device_id_type=MESH,
-            ).start()
-
-        for_devices(start)
-
-    def wait_turn(which, target):
-        wait_bytes(target.at[pl.ds(0, local * (devices - 1))], turn_in.at[which])
-
-    for m in range(local):
-        go_send[pl.ds(m, devices, stride=slot), :] = lanes(columns, m)
-    turn(0, go_send, go_recv, True)
-    for band in range(BANDS):
-        for c in range(2):
-            value = answer[band, c] + step_size[band] * search[band, c]
-            for m in range(local):
-                coeff[band, c, pl.ds(m, n, stride=local), :] = lanes(value, m)
-
     even = 2 * me
     frequency = jnp.where(
         pool == 0, even, jnp.where(pool == 1, jnp.where(me == 0, n // 2, even), even + 1)
@@ -617,25 +635,48 @@
     nonzero = (squared > 0).astype(f32)
     coulomb = 4.0 * math.pi * nonzero / (squared + (1.0 - nonzero))
 
-    wait_turn(0, go_recv)
+    wait_turn(0, go_recv.at[0])
+    sizes = []
+    for band in range(BANDS):
+        wait_turn(1 + band, go_recv.at[1 + band], local + 1)
+        sizes.append([])
+        for other in range(pools):
+            first = other * parts * slot + local
+            rows = go_recv[1 + band, pl.ds(first, parts, stride=slot), :]
+            values = unpack(jnp.sum(rows, axis=0, keepdims=True), 6)
+            sizes[band].append(finish_curvature(values[5], values[:5]))
     pieces = []
     for m in range(local):
-        piece = go_recv[pl.ds(m, parts, stride=slot), :]
-        for other in range(1, pools):
-            piece = piece + go_recv[pl.ds(other * parts * slot + m, parts, stride=slot), :]
+        piece = None
+        for other in range(pools):
+            rows = pl.ds(other * parts * slot + m, parts, stride=slot)
+            term = go_recv[0, rows, :]
+            for band in range(BANDS):
+                term = term + sizes[band][other] * go_recv[1 + band, rows, :]
+            piece = term if piece is None else piece + term
         back_send[0, pl.ds(m, parts, stride=slot), :] = piece
         pieces.append(piece)
-    turn(1, back_send.at[0], back_recv.at[0], False)
+    turn(3, back_send.at[0], back_recv.at[0], False)
 
 
     field = left_dot(basis_x[...], jnp.concatenate(pieces, axis=0))
     field = coulomb * right_dot(field, basis_z[0])
     field = left_dot(spread_x[...], right_dot(field, basis_z[1]))
     back_send[1] = field
-    turn(2, back_send.at[1], back_recv.at[1], False)
+    turn(4, back_send.at[1], back_recv.at[1], False)
+
+    for band in range(BANDS):
+        size = sum(jnp.where(pool == i, sizes[band][i], 0.0) for i in range(pools))
+        for c in range(2):
+            value = answer[band, c] + size * search[band, c]
+            for m in range(local):
+                coeff[band, c, pl.ds(m, n, stride=local), :] = lanes(value, m)
+    results = [(coeff, coeff_out), (density, density_out), (hxc, hxc_out)]
+    stores = [pltpu.make_async_copy(a, b, stored.at[i]) for i, (a, b) in enumerate(results)]
+    stores[0].start()
 
     for i, result in enumerate((density, hxc)):
-        wait_turn(1 + i, back_recv.at[i])
+        wait_turn(3 + i, back_recv.at[i])
         columns = [back_recv[i, pl.ds(m, devices, stride=slot), :] for m in range(local)]
         whole = left_dot(basis_y[1], jnp.concatenate(columns, axis=1))
         for m in range(local):
@@ -643,16 +684,19 @@
                 result[m] = lanes(whole, m)
             else:
                 result[m] = lanes(whole, m) + xc[m] * density[m]
+        stores[1 + i].start()
 
 
     for phase in range(2 * CG_STEPS + 1):
         for band in range(BANDS):
             for half in range(HALVES):
                 wait_bytes(half_bytes(phase, band, half), bulk_out.at[phase, band, half])
-    for slot in range(1 + BANDS):
-        wait_bytes(small_recv.at[slot, pl.ds(0, parts - 1)], small_out.at[slot])
-    for which in range(3):
-        wait_bytes(go_recv.at[pl.ds(0, local * (devices - 1))], turn_out.at[which])
+    for store in stores:
+        store.wait()
+    wait_bytes(small_recv.at[pl.ds(0, parts - 1)], small_out)
+    for which in range(5):
+        rows = local + 1 if which in (1, 2) else local
+        wait_bytes(go_recv.at[0, pl.ds(0, rows * (devices - 1))], turn_out.at[which])
 
 
 def hand_over(coeff, density, hxc, coeff_out, density_out, hxc_out, *scratch):
@@ -679,7 +723,6 @@
     wide = local * n
     phases = 2 * CG_STEPS + 1
     room = block + 8
-    slots = 1 + BANDS
     slot_rows = 2 * local * parts
     operands = [
         wave_coeff.reshape(BANDS, 2, n * local, n),
@@ -699,8 +742,13 @@
             jax.ShapeDtypeStruct((local, n, n), f32),
         ),
         in_specs=[anywhere, pl.BlockSpec(memory_space=pltpu.SMEM)] + [anywhere] * 10,
-        out_specs=(vmem, vmem, vmem),
-        scratch_shapes=[pltpu.VMEM(t.shape, t.dtype) for t in operands]
+        out_specs=(anywhere, anywhere, anywhere),
+        scratch_shapes=[
+            pltpu.VMEM(operands[0].shape, f32),
+            pltpu.VMEM((local, n, n), f32),
+            pltpu.VMEM((local, n, n), f32),
+        ]
+        + [pltpu.VMEM(t.shape, t.dtype) for t in operands]
         + [
             field,
             pltpu.VMEM((n, wide), f32),
@@ -715,18 +763,20 @@
             pltpu.VMEM((n, wide), f32),
             pltpu.VMEM((phases, BANDS, HALVES, parts, room, n), f32),
             pltpu.VMEM((phases, BANDS, HALVES, parts * room, n), f32),
-            pltpu.VMEM((slots, 1, n), f32),
-            pltpu.VMEM((slots, parts, 1, n), f32),
-            pltpu.VMEM((pools * slot_rows, n), f32),
-            pltpu.VMEM((pools * slot_rows, n), f32),
+            pltpu.VMEM((1, n), f32),
+            pltpu.VMEM((parts, 1, n), f32),
+            pltpu.VMEM((1 + BANDS, pools * slot_rows, n), f32),
+            pltpu.VMEM((1 + BANDS, pools * slot_rows, n), f32),
             pltpu.VMEM((2, slot_rows, n), f32),
             pltpu.VMEM((2, pools * slot_rows, n), f32),
             dma((11,)),
             dma((phases, BANDS, HALVES)),
             dma((phases, BANDS, HALVES)),
-            dma((slots,)),
-            dma((slots,)),
-            dma((3,)),
+            dma(()),
+            dma(()),
+            dma((5,)),
+            dma((5,)),
+            pltpu.SemaphoreType.REGULAR,
             dma((3,)),
         ],
         compiler_params=pltpu.CompilerParams(

time: 124 us -> 121 us (0.976)
  Pallas kernels: 123 us -> 120 us
    pallas_call x1, Pallas kernels: 121 us -> 118 us  [body(): pl.pallas_call(functools.partial(kernel, n, parts, pools), out_shape=(jax...]
where the time goes in v6:
time: 121 us
  Pallas kernels  120 us (99%)
    pallas_call x1, Pallas kernels, body(): pl.pallas_call(functools.partial(kernel, n, parts, pools), out_shape=(jax...  118 us

profile of v6, /device:TPU:1, one launch (start us, length us, event | category | flops | bytes accessed | tf_op | source)
XLA Modules:
  0.0 120.8 jit_solution(4747292998320834502)
XLA Ops:
  0.6 117.8 %shard_map.139 = (f32[2,2,512,128]{3,2,1,0:T(8,128)}, f32[4,128,128]{2,1,0:T(8,128)}, f32[4,128,128]{2,1,0:T(8,128)}) custom-call(f32[2,2,512,128]{3,2,1,0:T(8,128)} %bitcast.2, f32[1,2]{1,0:T(1,128)} %energy.1, f32[4,128,128]{2,1,0:T(8,128)} %potential_hbm.1, f32[4,128,128]{2,1,0:T(8,128)} %perturbation_hbm.1, f32[4,128,128]{2,1,0:T(8,128)} %xc_hbm.1, ...), custom_call_target="tpu_custom_call" | custom-call | tf_op jit(solution)/shard_map/pallas_call | solution.py:737
  118.5 2.2 %shard_map.140 = (f32[2,2,512,128]{3,2,1,0:T(8,128)}, f32[4,128,128]{2,1,0:T(8,128)}, f32[4,128,128]{2,1,0:T(8,128)}) custom-call(f32[2,2,512,128]{3,2,1,0:T(8,128)} %get-tuple-element.9.coeff, f32[4,128,128]{2,1,0:T(8,128)} %get-tuple-element.10.density, f32[4,128,128]{2,1,0:T(8,128)} %get-tuple-element.11.hxc), custom_call_target="tpu_custom_call" | custom-call | tf_op jit(solution)/shard_map/pallas_call | solution.py:787

commit v7 on v6

--- a/solution.py
+++ b/solution.py
@@ -184,25 +184,33 @@
         index = start + shift
         return jnp.where(index >= size, index - size, index)
 
-    def for_peers(act):
-        def step(shift, _):
+    def for_shifts(first, last, unroll, act):
+        odd = (last - first) % unroll
+        for shift in range(first, first + odd):
             act(turned(me, shift, parts))
+
+        def step(index, _):
+            shift = first + odd + index * unroll
+            for more in range(unroll):
+                act(turned(me, shift + more, parts))
             return 0
 
-        lax.fori_loop(parts // 2, parts, step, 0)
-        lax.fori_loop(1, parts // 2, step, 0)
+        lax.fori_loop(0, (last - first) // unroll, step, 0)
+
+    def for_peers(act, unroll=4):
+        for_shifts(parts // 2, parts, unroll, act)
+        for_shifts(1, parts // 2, unroll, act)
 
     def for_devices(act):
         for pool_shift in (2, 1, 3):
             other_pool = turned(pool, pool_shift, pools)
 
-            def step(shift, _, other_pool=other_pool):
-                act(turned(me, shift, parts), other_pool)
-                return 0
-
-            lax.fori_loop(parts // 2, parts, step, 0)
-            lax.fori_loop(0, parts // 2, step, 0)
-        for_peers(lambda other: act(other, pool))
+            def at_pool(other, other_pool=other_pool):
+                act(other, other_pool)
+
+            for_shifts(parts // 2, parts, 8, at_pool)
+            for_shifts(0, parts // 2, 8, at_pool)
+        for_peers(lambda other: act(other, pool), 8)
 
     barrier = pltpu.get_barrier_semaphore()
 
@@ -317,26 +325,26 @@
         rows = recv[phase, band, row_half(phase), pl.ds(block, parts, stride=room), :]
         return unpack(jnp.sum(rows, axis=0, keepdims=True), count)
 
-    def send_small(values):
+    def send_small(which, values):
         row = pack(values)
-        small_send[...] = row
-        small_recv[me] = row
+        small_send[which] = row
+        small_recv[which, me] = row
 
         def start(other):
             pltpu.make_async_remote_copy(
-                src_ref=small_send,
-                dst_ref=small_recv.at[me],
-                send_sem=small_out,
-                recv_sem=small_in,
+                src_ref=small_send.at[which],
+                dst_ref=small_recv.at[which, me],
+                send_sem=small_out.at[which],
+                recv_sem=small_in.at[which],
                 device_id={"fft": other},
                 device_id_type=MESH,
             ).start()
 
         for_peers(start)
 
-    def receive_small(count):
-        wait_bytes(small_recv.at[pl.ds(0, parts - 1)], small_in)
-        return unpack(jnp.sum(small_recv[...], axis=0), count)
+    def receive_small(which, count):
+        wait_bytes(small_recv.at[which, pl.ds(0, parts - 1)], small_in.at[which])
+        return unpack(jnp.sum(small_recv[which], axis=0), count)
 
 
     def along_z(real, imag, table):
@@ -438,7 +446,7 @@
             first_imag = space_wave[0, 1]
             overlaps.append(lane_sums(first_real * changed_real + first_imag * changed_imag))
             overlaps.append(lane_sums(first_real * changed_imag - first_imag * changed_real))
-            send_small(overlaps)
+            send_small(0, overlaps)
         send_reciprocal(1, band, changed_real, changed_imag)
 
     def products(band, real, imag):
@@ -468,7 +476,7 @@
     for band in range(BANDS):
         real, imag = receive_reciprocal(1, band)
         if band == 0:
-            same0, same1, cross_real, cross_imag = receive_small(4)
+            same0, same1, cross_real, cross_imag = receive_small(0, 4)
         if band == 0:
             m0_real, m0_imag, m1_real, m1_imag = same0, 0.0 * same0, cross_real, -cross_imag
         else:
@@ -522,26 +530,12 @@
     def wait_turn(which, target, rows=local):
         wait_bytes(target.at[pl.ds(0, rows * (devices - 1))], turn_in.at[which])
 
-    def send_columns(which, value):
-        columns = left_dot(basis_y[0], value)
+    def store_columns(which, columns):
         for m in range(local):
             go_send[which, pl.ds(m, devices, stride=slot), :] = lanes(columns, m)
 
-    def send_term(band, sums):
-        which = 1 + band
-        send_columns(which, overlap[band])
-        share = jnp.where(lane_id[:1] == 0, rho[band] * (1.0 / parts), 0.0)
-        go_send[which, pl.ds(local, devices, stride=slot), :] = jnp.broadcast_to(
-            pack(sums + [share]), (devices, n)
-        )
-        turn(which, go_send.at[which], go_recv.at[which], True, local + 1)
-
     for step in range(CG_STEPS):
         last = step + 1 == CG_STEPS
-        if last:
-            pl.semaphore_wait(met, pools - 1)
-            send_columns(0, total[...])
-            turn(0, go_send.at[0], go_recv.at[0], True)
         for band in range(BANDS):
             real, imag = ahead[band, 0], ahead[band, 1]
             sums = [kinetic_sum(band, real, imag, real, imag)] + products(band, real, imag)
@@ -574,8 +568,10 @@
                     search[band, c] = ahead[band, c]
                 else:
                     search[band, c] = ahead[band, c] + beta * search[band, c]
-            if last:
-                send_term(band, sums)
+            if last and band == 0:
+                send_small(1, sums)
+                base = left_dot(basis_y[0], total[...])
+                moved = left_dot(basis_y[0], overlap[band])
         if last:
             break
         for band in range(BANDS):
@@ -620,6 +616,17 @@
                 moved = size * search[band, c]
                 answer[band, c] = moved if step == 0 else answer[band, c] + moved
 
+    pl.semaphore_wait(met, pools - 1)
+    size_first = finish_curvature(rho[0], receive_small(1, 5))
+    store_columns(0, base + size_first * moved)
+    turn(0, go_send.at[0], go_recv.at[0], True)
+    store_columns(1, left_dot(basis_y[0], overlap[1]))
+    share = jnp.where(lane_id[:1] == 0, rho[1] * (1.0 / parts), 0.0)
+    go_send[1, pl.ds(local, devices, stride=slot), :] = jnp.broadcast_to(
+        pack(sums + [share]), (devices, n)
+    )
+    turn(1, go_send.at[1], go_recv.at[1], True, local + 1)
+
     even = 2 * me
     frequency = jnp.where(
         pool == 0, even, jnp.where(pool == 1, jnp.where(me == 0, n // 2, even), even + 1)
@@ -636,37 +643,35 @@
     coulomb = 4.0 * math.pi * nonzero / (squared + (1.0 - nonzero))
 
     wait_turn(0, go_recv.at[0])
+    wait_turn(1, go_recv.at[1], local + 1)
     sizes = []
-    for band in range(BANDS):
-        wait_turn(1 + band, go_recv.at[1 + band], local + 1)
-        sizes.append([])
-        for other in range(pools):
-            first = other * parts * slot + local
-            rows = go_recv[1 + band, pl.ds(first, parts, stride=slot), :]
-            values = unpack(jnp.sum(rows, axis=0, keepdims=True), 6)
-            sizes[band].append(finish_curvature(values[5], values[:5]))
+    for other in range(pools):
+        first = other * parts * slot + local
+        rows = go_recv[1, pl.ds(first, parts, stride=slot), :]
+        values = unpack(jnp.sum(rows, axis=0, keepdims=True), 6)
+        sizes.append(finish_curvature(values[5], values[:5]))
     pieces = []
     for m in range(local):
         piece = None
         for other in range(pools):
             rows = pl.ds(other * parts * slot + m, parts, stride=slot)
-            term = go_recv[0, rows, :]
-            for band in range(BANDS):
-                term = term + sizes[band][other] * go_recv[1 + band, rows, :]
+            term = go_recv[0, rows, :] + sizes[other] * go_recv[1, rows, :]
             piece = term if piece is None else piece + term
         back_send[0, pl.ds(m, parts, stride=slot), :] = piece
         pieces.append(piece)
-    turn(3, back_send.at[0], back_recv.at[0], False)
+    turn(2, back_send.at[0], back_recv.at[0], False)
 
 
     field = left_dot(basis_x[...], jnp.concatenate(pieces, axis=0))
     field = coulomb * right_dot(field, basis_z[0])
     field = left_dot(spread_x[...], right_dot(field, basis_z[1]))
     back_send[1] = field
-    turn(4, back_send.at[1], back_recv.at[1], False)
+    turn(3, back_send.at[1], back_recv.at[1], False)
 
     for band in range(BANDS):
-        size = sum(jnp.where(pool == i, sizes[band][i], 0.0) for i in range(pools))
+        size = size_first
+        if band == 1:
+            size = sum(jnp.where(pool == i, sizes[i], 0.0) for i in range(pools))
         for c in range(2):
             value = answer[band, c] + size * search[band, c]
             for m in range(local):
@@ -674,9 +679,15 @@
     results = [(coeff, coeff_out), (density, density_out), (hxc, hxc_out)]
     stores = [pltpu.make_async_copy(a, b, stored.at[i]) for i, (a, b) in enumerate(results)]
     stores[0].start()
+    for phase in range(2 * CG_STEPS + 1):
+        for band in range(BANDS):
+            for half in range(HALVES):
+                wait_bytes(half_bytes(phase, band, half), bulk_out.at[phase, band, half])
+    for slot_id in range(2):
+        wait_bytes(small_recv.at[slot_id, pl.ds(0, parts - 1)], small_out.at[slot_id])
 
     for i, result in enumerate((density, hxc)):
-        wait_turn(3 + i, back_recv.at[i])
+        wait_turn(2 + i, back_recv.at[i])
         columns = [back_recv[i, pl.ds(m, devices, stride=slot), :] for m in range(local)]
         whole = left_dot(basis_y[1], jnp.concatenate(columns, axis=1))
         for m in range(local):
@@ -687,15 +698,10 @@
         stores[1 + i].start()
 
 
-    for phase in range(2 * CG_STEPS + 1):
-        for band in range(BANDS):
-            for half in range(HALVES):
-                wait_bytes(half_bytes(phase, band, half), bulk_out.at[phase, band, half])
     for store in stores:
         store.wait()
-    wait_bytes(small_recv.at[pl.ds(0, parts - 1)], small_out)
-    for which in range(5):
-        rows = local + 1 if which in (1, 2) else local
+    for which in range(4):
+        rows = local + 1 if which == 1 else local
         wait_bytes(go_recv.at[0, pl.ds(0, rows * (devices - 1))], turn_out.at[which])
 
 
@@ -763,19 +769,19 @@
             pltpu.VMEM((n, wide), f32),
             pltpu.VMEM((phases, BANDS, HALVES, parts, room, n), f32),
             pltpu.VMEM((phases, BANDS, HALVES, parts * room, n), f32),
-            pltpu.VMEM((1, n), f32),
-            pltpu.VMEM((parts, 1, n), f32),
-            pltpu.VMEM((1 + BANDS, pools * slot_rows, n), f32),
-            pltpu.VMEM((1 + BANDS, pools * slot_rows, n), f32),
+            pltpu.VMEM((2, 1, n), f32),
+            pltpu.VMEM((2, parts, 1, n), f32),
+            pltpu.VMEM((2, pools * slot_rows, n), f32),
+            pltpu.VMEM((2, pools * slot_rows, n), f32),
             pltpu.VMEM((2, slot_rows, n), f32),
             pltpu.VMEM((2, pools * slot_rows, n), f32),
             dma((11,)),
             dma((phases, BANDS, HALVES)),
             dma((phases, BANDS, HALVES)),
-            dma(()),
-            dma(()),
-            dma((5,)),
-            dma((5,)),
+            dma((2,)),
+            dma((2,)),
+            dma((4,)),
+            dma((4,)),
             pltpu.SemaphoreType.REGULAR,
             dma((3,)),
         ],

time: 121 us -> 120 us (level)
  no operation moved by 1% of the time
where the time goes in v7:
time: 120 us
  Pallas kernels  119 us (99%)
    pallas_call x1, Pallas kernels, body(): pl.pallas_call(functools.partial(kernel, n, parts, pools), out_shape=(jax...  117 us

profile of v7, /device:TPU:1, one launch (start us, length us, event | category | flops | bytes accessed | tf_op | source)
XLA Modules:
  0.0 119.8 jit_solution(8186990432111474754)
XLA Ops:
  0.6 116.8 %shard_map.139 = (f32[2,2,512,128]{3,2,1,0:T(8,128)}, f32[4,128,128]{2,1,0:T(8,128)}, f32[4,128,128]{2,1,0:T(8,128)}) custom-call(f32[2,2,512,128]{3,2,1,0:T(8,128)} %bitcast.2, f32[1,2]{1,0:T(1,128)} %energy.1, f32[4,128,128]{2,1,0:T(8,128)} %potential_hbm.1, f32[4,128,128]{2,1,0:T(8,128)} %perturbation_hbm.1, f32[4,128,128]{2,1,0:T(8,128)} %xc_hbm.1, ...), custom_call_target="tpu_custom_call" | custom-call | tf_op jit(solution)/shard_map/pallas_call | solution.py:743
  117.5 2.2 %shard_map.140 = (f32[2,2,512,128]{3,2,1,0:T(8,128)}, f32[4,128,128]{2,1,0:T(8,128)}, f32[4,128,128]{2,1,0:T(8,128)}) custom-call(f32[2,2,512,128]{3,2,1,0:T(8,128)} %get-tuple-element.9.coeff, f32[4,128,128]{2,1,0:T(8,128)} %get-tuple-element.10.density, f32[4,128,128]{2,1,0:T(8,128)} %get-tuple-element.11.hxc), custom_call_target="tpu_custom_call" | custom-call | tf_op jit(solution)/shard_map/pallas_call | solution.py:793

commit v8 on v7

--- a/solution.py
+++ b/solution.py
@@ -541,6 +541,11 @@
             sums = [kinetic_sum(band, real, imag, real, imag)] + products(band, real, imag)
             if step > 0:
                 cross = kinetic_sum(band, real, imag, search[band, 0], search[band, 1])
+            if last and band == 1:
+                pl.semaphore_wait(met, pools - 1)
+                size_first = finish_curvature(rho[0], receive_small(1, 5))
+                store_columns(0, base + size_first * moved)
+                turn(0, go_send.at[0], go_recv.at[0], True)
             real, imag = receive_real(2 + 2 * step, band)
             (rho_new,) = bulk_row(2 + 2 * step, band, 1)
             if step > 0:
@@ -616,10 +621,6 @@
                 moved = size * search[band, c]
                 answer[band, c] = moved if step == 0 else answer[band, c] + moved
 
-    pl.semaphore_wait(met, pools - 1)
-    size_first = finish_curvature(rho[0], receive_small(1, 5))
-    store_columns(0, base + size_first * moved)
-    turn(0, go_send.at[0], go_recv.at[0], True)
     store_columns(1, left_dot(basis_y[0], overlap[1]))
     share = jnp.where(lane_id[:1] == 0, rho[1] * (1.0 / parts), 0.0)
     go_send[1, pl.ds(local, devices, stride=slot), :] = jnp.broadcast_to(
@@ -644,12 +645,18 @@
 
     wait_turn(0, go_recv.at[0])
     wait_turn(1, go_recv.at[1], local + 1)
-    sizes = []
+    gathered = []
     for other in range(pools):
         first = other * parts * slot + local
         rows = go_recv[1, pl.ds(first, parts, stride=slot), :]
-        values = unpack(jnp.sum(rows, axis=0, keepdims=True), 6)
-        sizes.append(finish_curvature(values[5], values[:5]))
+        gathered.append(jnp.sum(rows, axis=0, keepdims=True))
+    gathered = jnp.concatenate(gathered, axis=0)
+    lane = lane_id[:pools]
+    terms = jnp.where(lane == 0, gathered, 2.0 * gathered * gathered)
+    curvature = jnp.sum(jnp.where(lane < 1 + 2 * BANDS, terms, 0.0), axis=1, keepdims=True)
+    product = jnp.sum(jnp.where(lane == 1 + 2 * BANDS, gathered, 0.0), axis=1, keepdims=True)
+    quotient = product / curvature
+    sizes = [quotient[other : other + 1] for other in range(pools)]
     pieces = []
     for m in range(local):
         piece = None

time: 120 us -> 119 us (level)
  no operation moved by 1% of the time
where the time goes in v8:
time: 119 us
  Pallas kernels  119 us (100%)
    pallas_call x1, Pallas kernels, body(): pl.pallas_call(functools.partial(kernel, n, parts, pools), out_shape=(jax...  116 us

profile of v8, /device:TPU:1, one launch (start us, length us, event | category | flops | bytes accessed | tf_op | source)
XLA Modules:
  0.0 119.3 jit_solution(9665537170072102893)
XLA Ops:
  0.6 116.4 %shard_map.139 = (f32[2,2,512,128]{3,2,1,0:T(8,128)}, f32[4,128,128]{2,1,0:T(8,128)}, f32[4,128,128]{2,1,0:T(8,128)}) custom-call(f32[2,2,512,128]{3,2,1,0:T(8,128)} %bitcast.2, f32[1,2]{1,0:T(1,128)} %energy.1, f32[4,128,128]{2,1,0:T(8,128)} %potential_hbm.1, f32[4,128,128]{2,1,0:T(8,128)} %perturbation_hbm.1, f32[4,128,128]{2,1,0:T(8,128)} %xc_hbm.1, ...), custom_call_target="tpu_custom_call" | custom-call | tf_op jit(solution)/shard_map/pallas_call | solution.py:750
  117.0 2.2 %shard_map.140 = (f32[2,2,512,128]{3,2,1,0:T(8,128)}, f32[4,128,128]{2,1,0:T(8,128)}, f32[4,128,128]{2,1,0:T(8,128)}) custom-call(f32[2,2,512,128]{3,2,1,0:T(8,128)} %get-tuple-element.9.coeff, f32[4,128,128]{2,1,0:T(8,128)} %get-tuple-element.10.density, f32[4,128,128]{2,1,0:T(8,128)} %get-tuple-element.11.hxc), custom_call_target="tpu_custom_call" | custom-call | tf_op jit(solution)/shard_map/pallas_call | solution.py:800

commit v9 on v8

--- a/solution.py
+++ b/solution.py
@@ -111,6 +111,7 @@
     n,
     parts,
     pools,
+    grid,
     raw_hbm,
     energy,
     potential_hbm,
@@ -184,22 +185,28 @@
         index = start + shift
         return jnp.where(index >= size, index - size, index)
 
-    def for_shifts(first, last, unroll, act):
-        odd = (last - first) % unroll
-        for shift in range(first, first + odd):
-            act(turned(me, shift, parts))
-
+    size_z, size_x, size_c = grid
+    plane = size_x * size_c
+    my_z, my_x, my_c = me // plane, lax.rem(me // size_c, size_x), lax.rem(me, size_c)
+    in_plane = [
+        turned(my_x, dx, size_x) * size_c + turned(my_c, dc, size_c)
+        for dx in reversed(range(size_x))
+        for dc in reversed(range(size_c))
+    ]
+
+    def for_planes(first, act):
         def step(index, _):
-            shift = first + odd + index * unroll
-            for more in range(unroll):
-                act(turned(me, shift + more, parts))
+            base = turned(my_z, size_z - 1 - index, size_z) * plane
+            for place in in_plane:
+                act(base + place)
             return 0
 
-        lax.fori_loop(0, (last - first) // unroll, step, 0)
-
-    def for_peers(act, unroll=4):
-        for_shifts(parts // 2, parts, unroll, act)
-        for_shifts(1, parts // 2, unroll, act)
+        lax.fori_loop(0, size_z - first, step, 0)
+
+    def for_peers(act):
+        for_planes(1, act)
+        for place in in_plane[:-1]:
+            act(my_z * plane + place)
 
     def for_devices(act):
         for pool_shift in (2, 1, 3):
@@ -208,9 +215,8 @@
             def at_pool(other, other_pool=other_pool):
                 act(other, other_pool)
 
-            for_shifts(parts // 2, parts, 8, at_pool)
-            for_shifts(0, parts // 2, 8, at_pool)
-        for_peers(lambda other: act(other, pool), 8)
+            for_planes(0, at_pool)
+        for_peers(lambda other: act(other, pool))
 
     barrier = pltpu.get_barrier_semaphore()
 
@@ -737,6 +743,7 @@
     phases = 2 * CG_STEPS + 1
     room = block + 8
     slot_rows = 2 * local * parts
+    grid = (4, 4, 2) if parts == 32 else (1, parts // 2, 2)
     operands = [
         wave_coeff.reshape(BANDS, 2, n * local, n),
         local_potential,
@@ -748,7 +755,7 @@
     field = pltpu.VMEM((BANDS, 2, n, wide), f32)
     dma = pltpu.SemaphoreType.DMA
     coeff, density, hxc = pl.pallas_call(
-        functools.partial(kernel, n, parts, pools),
+        functools.partial(kernel, n, parts, pools, grid),
         out_shape=(
             jax.ShapeDtypeStruct(operands[0].shape, f32),
             jax.ShapeDtypeStruct((local, n, n), f32),

time: 119 us -> 119 us (level)
  no operation moved by 1% of the time
where the time goes in v9:
time: 119 us
  Pallas kernels  118 us (99%)
    pallas_call x1, Pallas kernels, body(): pl.pallas_call(functools.partial(kernel, n, parts, pools, grid), out_shap...  116 us

profile of v9, /device:TPU:1, one launch (start us, length us, event | category | flops | bytes accessed | tf_op | source)
XLA Modules:
  0.0 119.1 jit_solution(2524089507845208107)
XLA Ops:
  0.6 116.1 %shard_map.139 = (f32[2,2,512,128]{3,2,1,0:T(8,128)}, f32[4,128,128]{2,1,0:T(8,128)}, f32[4,128,128]{2,1,0:T(8,128)}) custom-call(f32[2,2,512,128]{3,2,1,0:T(8,128)} %bitcast.2, f32[1,2]{1,0:T(1,128)} %energy.1, f32[4,128,128]{2,1,0:T(8,128)} %potential_hbm.1, f32[4,128,128]{2,1,0:T(8,128)} %perturbation_hbm.1, f32[4,128,128]{2,1,0:T(8,128)} %xc_hbm.1, ...), custom_call_target="tpu_custom_call" | custom-call | tf_op jit(solution)/shard_map/pallas_call | solution.py:757
  116.8 2.2 %shard_map.140 = (f32[2,2,512,128]{3,2,1,0:T(8,128)}, f32[4,128,128]{2,1,0:T(8,128)}, f32[4,128,128]{2,1,0:T(8,128)}) custom-call(f32[2,2,512,128]{3,2,1,0:T(8,128)} %get-tuple-element.9.coeff, f32[4,128,128]{2,1,0:T(8,128)} %get-tuple-element.10.density, f32[4,128,128]{2,1,0:T(8,128)} %get-tuple-element.11.hxc), custom_call_target="tpu_custom_call" | custom-call | tf_op jit(solution)/shard_map/pallas_call | solution.py:807
